TPU v7x, 256 devices: a whole 4x4x8 slice. The times are simulated.
256 devices in a mesh: seq: 32 (over y, z), row: 2 (over x_hi), col: 4 (over x_lo, core).
Axes of the slice: x: 4 (x_hi: 2, x_lo: 2; x = x_hi * 2 + x_lo), y: 4, z: 8, core: 2. Of those that a mesh axis runs over, the one named last changes fastest.
Arguments:
- tokens: bfloat16 [8192, 12288], P('seq', ('row', 'col')), may hold values from -24 to 24
- input_weight: bfloat16 [12288, 1536], P('row', 'col'), may hold values from -0.078125 to 0.078125
- output_weight: bfloat16 [512, 12288], P('col'), may hold values from -0.25 to 0.25
- output_cotangent: bfloat16 [8192, 12288], P(('seq', 'row'), 'col'), may hold values from -1.1953125 to 1.1953125
Outputs:
- layer_output: bfloat16 [8192, 12288], P(('seq', 'row'), 'col')
- input_grad: bfloat16 [8192, 12288], P('seq', ('row', 'col'))
All inputs are finite; a program needn't handle non-finite values.
Results may differ from a plain program's by a relative error of at most 0.0364.
The roundings to bfloat16 on the way count: a program that leaves them out, or rounds other values in their place, can miss the bound.
Values may be sent and summed in bfloat16 or wider, within the bound.
A program may use at most 128 MiB of HBM per device.

v0:
```python
import math

import jax
import jax.numpy as jnp
from jax import lax
from jax.sharding import PartitionSpec as P

HEAD = 128


masked_score = -1e30


def shifted(block, axis, distance):
    devices = range(lax.axis_size(axis))
    route = [(i - distance, i) for i in devices if i - distance in devices]
    return lax.ppermute(block, axis, route)


def from_behind(value, axis, steps):
    count = lax.axis_size(axis)
    pairs = [(source, (source + steps) % count) for source in range(count)]
    return lax.ppermute(value, axis, pairs)


def attend_block(running, queries, key_values, key_pos, query_pos, factor):
    largest, total_sum, mixed_sum = running
    scores = (
        jnp.einsum("hqd,hkd->hqk", queries, key_values[0], preferred_element_type=jnp.float32)
        * factor
    )
    allowed = key_pos[None, :] <= query_pos[:, None]
    scores = jnp.where(allowed[None], scores, masked_score)
    new_largest = jnp.maximum(largest, jnp.max(scores, axis=-1))
    weights = jnp.exp(scores - new_largest[..., None])
    shrink = jnp.exp(largest - new_largest)
    total_sum = total_sum * shrink + jnp.sum(weights, axis=-1)
    mixed_sum = mixed_sum * shrink[..., None] + jnp.einsum(
        "hqk,hkd->hqd",
        weights.astype(jnp.bfloat16),
        key_values[1],
        preferred_element_type=jnp.float32,
    )
    return (new_largest, total_sum, mixed_sum)


def gradient_block(queries, upstream, logsum, row_delta, query_pos, key_values, key_pos, factor):
    scores = (
        jnp.einsum("hqd,hkd->hqk", queries, key_values[0], preferred_element_type=jnp.float32)
        * factor
    )
    allowed = key_pos[None, :] <= query_pos[:, None]
    scores = jnp.where(allowed[None], scores, masked_score)
    probabilities = jnp.exp(scores - logsum[..., None])
    prob_grad = jnp.einsum(
        "hqd,hkd->hqk", upstream, key_values[1], preferred_element_type=jnp.float32
    )
    score_grad = (probabilities * (prob_grad - row_delta[..., None])).astype(jnp.bfloat16)
    query_grad = jnp.einsum(
        "hqk,hkd->hqd", score_grad, key_values[0], preferred_element_type=jnp.float32
    )
    key_grad = jnp.einsum("hqk,hqd->hkd", score_grad, queries, preferred_element_type=jnp.float32)
    value_grad = jnp.einsum(
        "hqk,hqd->hkd",
        probabilities.astype(jnp.bfloat16),
        upstream,
        preferred_element_type=jnp.float32,
    )
    return (query_grad, jnp.stack([key_grad, value_grad]))


def body(tokens, input_weight, output_weight, output_cotangent):
    seq_count = lax.axis_size("seq")
    seq_id = lax.axis_index("seq")
    row_id = lax.axis_index("row")
    tok_dev = tokens.shape[0]
    local_width = input_weight.shape[1]
    local_heads = local_width // (3 * HEAD)
    half_rows = tok_dev // lax.axis_size("row")
    factor = 1.0 / math.sqrt(HEAD)
    beyond_end = seq_count * tok_dev
    partial_value = jnp.dot(
        lax.all_gather(tokens, "col", axis=1, tiled=True),
        input_weight,
        preferred_element_type=jnp.float32,
    )
    packed = lax.psum_scatter(partial_value, "row", scatter_dimension=0, tiled=True).astype(
        jnp.bfloat16
    )
    shaped = jnp.transpose(packed.reshape(half_rows, local_heads, 3, HEAD), (2, 1, 0, 3))
    queries = shaped[0]
    own_pair = lax.all_gather(shaped[1:], "row", axis=2, tiled=True)
    offsets = jnp.arange(tok_dev, dtype=jnp.int32)
    row_offsets = jnp.arange(half_rows, dtype=jnp.int32)
    query_pos = seq_id * tok_dev + row_id * half_rows + row_offsets
    own_key_pos = seq_id * tok_dev + offsets

    def arriving_pos(turn_index):
        source = seq_id - turn_index
        return jnp.where(source >= 0, source * tok_dev + offsets, beyond_end + offsets)

    start_state = (
        jnp.full((local_heads, half_rows), masked_score, jnp.float32),
        jnp.zeros((local_heads, half_rows), jnp.float32),
        jnp.zeros((local_heads, half_rows, HEAD), jnp.float32),
    )
    running = attend_block(start_state, queries, own_pair, own_key_pos, query_pos, factor)

    def forward_turn(turn_index, carry):
        running, key_values = carry
        key_values = shifted(key_values, "seq", 1)
        running = attend_block(
            running, queries, key_values, arriving_pos(turn_index), query_pos, factor
        )
        return (running, key_values)

    running, unused = lax.fori_loop(1, seq_count, forward_turn, (running, own_pair))
    largest, total_sum, mixed_sum = running
    attended = (mixed_sum / total_sum[..., None]).astype(jnp.bfloat16)
    logsum = largest + jnp.log(total_sum)
    flattened = jnp.transpose(attended, (1, 0, 2)).reshape(half_rows, local_heads * HEAD)
    head_terms = jnp.dot(flattened, output_weight, preferred_element_type=jnp.float32)
    layer_output = lax.psum_scatter(head_terms, "col", scatter_dimension=1, tiled=True).astype(
        jnp.bfloat16
    )
    upstream = lax.dot_general(
        lax.all_gather(output_cotangent, "col", axis=1, tiled=True),
        output_weight,
        (((1,), (1,)), ((), ())),
        preferred_element_type=jnp.float32,
    ).astype(jnp.bfloat16)
    upstream = jnp.transpose(upstream.reshape(half_rows, local_heads, HEAD), (1, 0, 2))
    row_delta = jnp.sum(upstream.astype(jnp.float32) * attended.astype(jnp.float32), axis=-1)
    query_grad, key_acc = gradient_block(
        queries, upstream, logsum, row_delta, query_pos, own_pair, own_key_pos, factor
    )

    def key_turn(turn_index, carry):
        key_values, key_acc, query_grad = carry
        key_values = shifted(key_values, "seq", 1)
        key_acc = from_behind(key_acc, "seq", 1)
        more_grad, more_keys = gradient_block(
            queries,
            upstream,
            logsum,
            row_delta,
            query_pos,
            key_values,
            arriving_pos(turn_index),
            factor,
        )
        return (key_values, key_acc + more_keys, query_grad + more_grad)

    unused, key_acc, query_grad = lax.fori_loop(
        1, seq_count + 1, key_turn, (own_pair, key_acc, query_grad)
    )
    key_sums = lax.psum_scatter(key_acc, "row", scatter_dimension=2, tiled=True)
    grads = jnp.stack([query_grad * factor, key_sums[0] * factor, key_sums[1]])
    packed_grad = (
        jnp.transpose(grads, (2, 1, 0, 3)).reshape(half_rows, local_width).astype(jnp.bfloat16)
    )
    gathered = lax.all_gather(packed_grad, "row", axis=0, tiled=True)
    input_terms = lax.dot_general(
        gathered, input_weight, (((1,), (1,)), ((), ())), preferred_element_type=jnp.float32
    )
    input_grad = lax.psum_scatter(input_terms, "col", scatter_dimension=1, tiled=True).astype(
        jnp.bfloat16
    )
    return (layer_output, input_grad)


def solution(mesh):
    return jax.shard_map(
        body,
        mesh=mesh,
        in_specs=(
            P("seq", ("row", "col")),
            P("row", "col"),
            P("col", None),
            P(("seq", "row"), "col"),
        ),
        out_specs=(P(("seq", "row"), "col"), P("seq", ("row", "col"))),
        check_vma=False,
    )
```

profile of v0, /device:TPU:1, one launch (start us, length us, event | category | flops | bytes accessed | tf_op | source)
XLA Modules:
  0.0 1129.9 jit_solution(7660588938565493313)
XLA Ops:
  8.0 46.5 %all-gather.3.cloned.1.call-done = bf16[256,6144]{1,0:T(8,128)(2,1)} async-done(((bf16[256,1536]{1,0:T(8,128)(2,1)}), bf16[256,6144]{1,0:T(8,128)(2,1)}) %all-gather.3.cloned.1.call-update) | async-done | bytes 3145744 | tf_op jit(solution)/shard_map/all_gather | solution.py:83
  54.4 5.8 fusion.51
  61.1 19.5 %reduce-scatter.5.cloned.1.call-done = f32[128,384]{1,0:T(8,128)} async-done(((f32[256,384]{1,0:T(8,128)}), f32[128,384]{1,0:T(8,128)}) %reduce-scatter.5.cloned.1.call-update) | async-done | bytes 196624 | tf_op jit(solution)/shard_map/reduce_scatter | solution.py:87
  83.1 5.3 all_gather.13
  92.2 299.0 %while.40 = (s32[]{:T(128)}, f32[1,128]{1,0:T(1,128)S(1)}, f32[1,128]{1,0:T(1,128)S(1)}, f32[1,128,128]{2,1,0:T(8,128)S(1)}, bf16[2,1,256,128]{3,2,1,0:T(8,128)(...) while((s32[]{:T(128)}, f32[1,128]{1,0:T(1,128)S(1)}, ...), condition=%wide.region_6.7_spmd.clone.clone, body=%wide.region_3.6_spmd.clone.clone.sunk | while | flops 17073412 | bytes 1486015 | solution.py:117
  161.3 5.2 collective-permute-start
  200.2 5.2 collective-permute-start
  257.2 5.5 collective-permute-start
  267.9 5.2 collective-permute-start
  277.7 5.8 collective-permute-start
  287.9 6.1 collective-permute-start
  298.3 5.6 collective-permute-start
  308.4 6.0 collective-permute-start
  318.7 5.5 collective-permute-start
  328.7 5.6 collective-permute-start
  338.7 5.6 collective-permute-start
  348.7 6.1 collective-permute-start
  359.2 5.8 collective-permute-start
  369.4 5.8 collective-permute-start
  379.6 6.1 collective-permute-start
  399.5 506.9 %while.41 = (s32[]{:T(128)}, bf16[2,1,256,128]{3,2,1,0:T(8,128)(2,1)}, f32[2,1,256,128]{3,2,1,0:T(8,128)}, f32[1,128,128]{2,1,0:T(8,128)}, s32[]{:T(128)}, /*ind...) while((s32[]{:T(128)}, ...), condition=%wide.region_10.11_spmd.clone.clone, body=%wide.region_9.10_spmd.clone.clone.sunk | while | flops 42353540 | bytes 3936503 | solution.py:154
  399.5 6.2 collective-permute-start.1
  416.6 6.1 collective-permute-start.1
  433.3 5.5 collective-permute-start.1
  449.3 6.1 collective-permute-start.1
  541.0 5.4 collective-permute-start.1
  572.2 5.2 collective-permute-start.1
  913.8 71.2 %reduce-scatter.9.cloned.1.call-done = f32[2,1,128,128]{2,3,0,1:T(8,128)} async-done(((f32[2,1,256,128]{2,3,0,1:T(8,128)}), f32[2,1,128,128]{2,3,0,1:T(8,128)}) %reduce-scatter.9.cloned.1.call-update) | async-done | bytes 131088 | tf_op jit(solution)/shard_map/reduce_scatter | solution.py:157
  986.7 5.7 all_gather.15
  992.4 7.4 fusion.52
  999.8 52.4 %reduce-scatter.7.cloned.1.call-done = f32[128,3072]{1,0:T(8,128)} async-done(((f32[128,12288]{1,0:T(8,128)}), f32[128,3072]{1,0:T(8,128)}) %reduce-scatter.7.cloned.1.call-update) | async-done | bytes 1572880 | tf_op jit(solution)/shard_map/reduce_scatter | solution.py:123
  1054.6 66.1 %reduce-scatter.11.cloned.1.call-done = f32[256,1536]{1,0:T(8,128)} async-done(((f32[256,6144]{1,0:T(8,128)}), f32[256,1536]{1,0:T(8,128)}) %reduce-scatter.11.cloned.1.call-update) | async-done | bytes 1572880 | tf_op jit(solution)/shard_map/reduce_scatter | solution.py:166
  (793 shorter events, 712.7 us)
Async XLA Ops:
  7.2 47.3 %all-gather.3.cloned.1.call-start = ((), (), s32[]{:S(2)}) async-start(), calls=%async_computation.4 | async-start | bytes 3932160 | tf_op jit(solution)/shard_map/all_gather | solution.py:83
  7.9 72.7 %reduce-scatter.5.cloned.1.call-start = ((), (), s32[]{:S(2)}) async-start(), calls=%async_computation.5 | async-start | bytes 589824 | tf_op jit(solution)/shard_map/reduce_scatter | solution.py:87
  60.3 331.1 %all-gather.5.cloned.1.call-start = ((), (), s32[]{:S(2)}) async-start(), calls=%async_computation.7 | async-start | bytes 3932160 | tf_op jit(solution)/shard_map/all_gather | solution.py:127
  61.0 924.0 %reduce-scatter.9.cloned.1.call-start = ((), (), s32[]{:S(2)}) async-start(), calls=%async_computation.8 | async-start | bytes 393216 | tf_op jit(solution)/shard_map/reduce_scatter | solution.py:157
  399.5 10.2 collective-permute-start.1
  405.7 10.1 collective-permute-start.2
  449.3 10.1 collective-permute-start.1
  455.4 10.0 collective-permute-start.2
  485.0 10.0 collective-permute-start.2
  577.4 10.3 collective-permute-start.2
  592.6 10.3 collective-permute-start.2
  608.3 10.3 collective-permute-start.2
  624.3 10.3 collective-permute-start.2
  640.2 10.3 collective-permute-start.2
  656.2 10.3 collective-permute-start.2
  672.1 10.3 collective-permute-start.2
  688.1 10.3 collective-permute-start.2
  704.0 10.3 collective-permute-start.2
  720.0 10.3 collective-permute-start.2
  735.9 10.3 collective-permute-start.2
  751.9 10.3 collective-permute-start.2
  767.8 10.3 collective-permute-start.2
  783.8 10.3 collective-permute-start.2
  799.7 10.3 collective-permute-start.2
  815.7 10.3 collective-permute-start.2
  831.6 10.3 collective-permute-start.2
  847.6 10.3 collective-permute-start.2
  863.5 10.3 collective-permute-start.2
  879.5 10.3 collective-permute-start.2
  895.4 10.3 collective-permute-start.2
  908.3 144.0 %reduce-scatter.7.cloned.1.call-start = ((), (), s32[]{:S(2)}) async-start(), calls=%async_computation.6 | async-start | bytes 7864320 | tf_op jit(solution)/shard_map/reduce_scatter | solution.py:123
  912.8 207.8 %reduce-scatter.11.cloned.1.call-start = ((), (), s32[]{:S(2)}) async-start(), calls=%async_computation.9 | async-start | bytes 7864320 | tf_op jit(solution)/shard_map/reduce_scatter | solution.py:166
  (75 other events, 968.9 us)
Sparse Core Ops, SparseCore 0:
  9.8 44.5 all-gather.2
  60.4 20.1 reduce-scatter.4
  82.6 40.2 all-gather.4
  908.4 76.5 reduce-scatter.8
  987.4 64.7 reduce-scatter.6
  1054.6 66.0 reduce-scatter.10
where the time goes:
time: 1140 us; the launch traced here: 1130 us
  starting transfers between devices  441 us (39%)
  waiting for transfers between devices  337 us (30%)
  matrix products  235 us (21%)
  local copies, waits for them, and re-layouts  50 us (4%)
  other arithmetic  38.8 us (3%)
  between operations  14.3 us (1%)
    ppermute x63, starting transfers between devices, shifted(): return lax.ppermute(block, axis, route)  317 us
    ppermute x32, starting transfers between devices, from_behind(): return lax.ppermute(value, axis, pairs)  123 us
    ppermute x63, waiting for transfers between devices, shifted(): return lax.ppermute(block, axis, route)  73.5 us
    reduce_scatter x1, waiting for transfers between devices, body(): key_sums = lax.psum_scatter(key_acc, 'row', scatter_dimension=2, tiled=True)  71.2 us
    reduce_scatter x1, waiting for transfers between devices, body(): lax.psum_scatter(input_terms, 'col', scatter_dimension=1, tiled=True)  66.1 us
    reduce_scatter x1, waiting for transfers between devices, body(): lax.psum_scatter(head_terms, 'col', scatter_dimension=1, tiled=True)  52.4 us
    dot_general x33, matrix products, gradient_block(): jnp.einsum('hqk,hkd->hqd', score_grad, key_values[0], preferred_element_t...  52.2 us
    all_gather x1, waiting for transfers between devices, body(): lax.all_gather(tokens, 'col', axis=1, tiled=True)  46.5 us
  transfers between devices with their start and end apart: 101, of which 60 were waited for; matrix products, arithmetic and copies ran while one was open for 25% of the time, Pallas kernels for 0%

commit v1 on v0

v1 whole, which is shorter than its diff:
```python
import functools
import math

import jax
import jax.numpy as jnp
from jax import lax
from jax.experimental import pallas as pl
from jax.experimental.pallas import tpu as pltpu
from jax.sharding import PartitionSpec as P

HEAD = 128
MESH = pl.DeviceIdType.MESH
masked_score = -1e30
BF = jnp.bfloat16
F32 = jnp.float32
NJ = 4


def remote(src, dst, send_sem, recv_sem, device):
    return pltpu.make_async_remote_copy(
        src_ref=src,
        dst_ref=dst,
        send_sem=send_sem,
        recv_sem=recv_sem,
        device_id=device,
        device_id_type=MESH,
    )


def greet(devices):
    barrier = pltpu.get_barrier_semaphore()
    for device in devices:
        pl.semaphore_signal(barrier, inc=1, device_id=device, device_id_type=MESH)
    pl.semaphore_wait(barrier, len(devices))


def dot_nt(a, b):
    return lax.dot_general(a, b, (((1,), (1,)), ((), ())), preferred_element_type=F32)


def dot_tn(a, b):
    return lax.dot_general(a, b, (((0,), (0,)), ((), ())), preferred_element_type=F32)


def flip(c, bits):
    low, high = lax.rem(c, 2), c // 2
    if bits & 1:
        low = 1 - low
    if bits & 2:
        high = 1 - high
    return high * 2 + low


def seed_kernel(ns, w_ref, wo_ref, sw_ref, swo_ref, bw, bwo, send, recv):
    s, r, c = lax.axis_index("seq"), lax.axis_index("row"), lax.axis_index("col")
    depth = w_ref.shape[0] // 4
    piece = depth // ns
    width = wo_ref.shape[1] // 4
    part = width // NJ
    ni = ns // NJ
    rows = HEAD // ni
    j, i = s // ni, lax.rem(s, ni)
    peers = [flip(c, 2), flip(c, 3)]
    greet([(s, r, p) for p in peers])
    copies = []
    for h, p in enumerate(peers):
        copies.append(
            remote(
                w_ref.at[pl.ds(pl.multiple_of(p * depth + s * piece, 16), piece), :],
                bw.at[h],
                send.at[0, h],
                recv.at[0, h],
                (s, r, p),
            )
        )
        copies.append(
            remote(
                wo_ref.at[
                    pl.ds(pl.multiple_of(i * rows, 16), rows),
                    pl.ds(pl.multiple_of(p * width + j * part, 128), part),
                ],
                bwo.at[h],
                send.at[1, h],
                recv.at[1, h],
                (s, r, p),
            )
        )
    for copy in copies:
        copy.start()
    for copy in copies:
        copy.wait()
    n = bw.shape[2]
    for h in range(2):
        sw_ref[:, h * n : (h + 1) * n] = bw[h]
        swo_ref[:, h * part : (h + 1) * part] = bwo[h]


def seeds(w, wo):
    ns = lax.axis_size("seq")
    depth, n = w.shape[0] // 4, w.shape[1]
    part = wo.shape[1] // 4 // NJ
    rows = HEAD // (ns // NJ)
    vm = pl.BlockSpec(memory_space=pltpu.VMEM)
    return pl.pallas_call(
        functools.partial(seed_kernel, ns),
        out_shape=(
            jax.ShapeDtypeStruct((depth // ns, 2 * n), BF),
            jax.ShapeDtypeStruct((rows, 2 * part), BF),
        ),
        in_specs=[pl.BlockSpec(memory_space=pl.ANY)] * 2,
        out_specs=(vm, vm),
        scratch_shapes=[
            pltpu.VMEM((2, depth // ns, n), BF),
            pltpu.VMEM((2, rows, part), BF),
            pltpu.SemaphoreType.DMA((2, 2)),
            pltpu.SemaphoreType.DMA((2, 2)),
        ],
        compiler_params=pltpu.CompilerParams(collective_id=0, has_side_effects=True),
        name="seeds",
    )(w, wo)


CHUNKS = 4


def proj_kernel(
    t_ref, w_ref, packed_ref, wsib_ref, tbuf, wv, psend, precv, wsem, lsem, sib, snd, rcv, psnd, prcv
):
    s, r, c = lax.axis_index("seq"), lax.axis_index("row"), lax.axis_index("col")
    depth = t_ref.shape[1]
    half = t_ref.shape[0] // 2
    step = 2 * half // CHUNKS
    sibling, across, far = flip(c, 1), flip(c, 2), flip(c, 3)
    to_sib, to_across, to_row = (s, r, sibling), (s, r, across), (s, 1 - r, c)

    wcopy = pltpu.make_async_copy(w_ref, wv, wsem)
    wcopy.start()

    def rows_of(k):
        hk = CHUNKS // 2
        start = (1 - r) * half + k * step if k < hk else r * half + (k - hk) * step
        return pl.ds(pl.multiple_of(start, step), step)

    own = pltpu.make_async_copy(t_ref, tbuf.at[c], lsem)
    own.start()
    greet([to_sib, to_across, to_row])

    def token_copy(kind, k):
        rows = rows_of(k)
        if kind == 0:
            return remote(t_ref.at[rows], tbuf.at[c, rows], snd.at[0, k], rcv.at[0, k], to_across)
        if kind == 1:
            return remote(t_ref.at[rows], tbuf.at[c, rows], snd.at[1, k], rcv.at[1, k], to_sib)
        return remote(
            tbuf.at[across, rows], tbuf.at[across, rows], snd.at[2, k], rcv.at[2, k], to_sib
        )

    def arrival(kind, k):
        rows = rows_of(k)
        slot = (across, sibling, far)[kind]
        return remote(
            tbuf.at[slot, rows], tbuf.at[slot, rows], snd.at[kind, k], rcv.at[kind, k], to_sib
        )

    for k in range(CHUNKS):
        token_copy(0, k).start()
        token_copy(1, k).start()
    wide = remote(
        w_ref.at[pl.ds(pl.multiple_of(sibling * depth, 16), depth), :],
        wsib_ref,
        sib.at[0],
        sib.at[1],
        to_sib,
    )
    wide.start()
    own.wait()
    wcopy.wait()

    def product(slot, rows):
        return jnp.dot(
            tbuf[slot, rows, :],
            wv[pl.ds(pl.multiple_of(slot * depth, 16), depth), :],
            preferred_element_type=F32,
        )

    def part_copy(k):
        rows = pl.ds(k * step, step)
        return remote(psend.at[rows], precv.at[rows], psnd.at[k], prcv.at[k], to_row)

    for k in range(CHUNKS):
        rows = rows_of(k)
        arrival(0, k).wait_recv()
        token_copy(2, k).start()
        arrival(1, k).wait_recv()
        acc = product(c, rows) + product(sibling, rows) + product(across, rows)
        arrival(2, k).wait_recv()
        acc = acc + product(far, rows)
        hk = CHUNKS // 2
        if k < hk:
            psend[pl.ds(k * step, step), :] = acc
            part_copy(k).start()
        else:
            part_copy(k - hk).wait_recv()
            out = pl.ds((k - hk) * step, step)
            packed_ref[out, :] = (acc + precv[out, :]).astype(BF)
    for k in range(CHUNKS):
        for kind in range(3):
            token_copy(kind, k).wait_send()
    for k in range(CHUNKS // 2):
        part_copy(k).wait_send()
    wide.wait()


def project(tokens, w):
    rows, depth = tokens.shape
    n = w.shape[1]
    half = rows // 2
    hbm = pl.BlockSpec(memory_space=pl.ANY)
    return pl.pallas_call(
        proj_kernel,
        out_shape=(
            jax.ShapeDtypeStruct((half, n), BF),
            jax.ShapeDtypeStruct((depth, n), BF),
        ),
        in_specs=[hbm, hbm],
        out_specs=(pl.BlockSpec(memory_space=pltpu.VMEM), hbm),
        scratch_shapes=[
            pltpu.VMEM((4, rows, depth), BF),
            pltpu.VMEM(w.shape, BF),
            pltpu.VMEM((half, n), F32),
            pltpu.VMEM((half, n), F32),
            pltpu.SemaphoreType.DMA,
            pltpu.SemaphoreType.DMA,
            pltpu.SemaphoreType.DMA((2,)),
            pltpu.SemaphoreType.DMA((3, CHUNKS)),
            pltpu.SemaphoreType.DMA((3, CHUNKS)),
            pltpu.SemaphoreType.DMA((CHUNKS // 2,)),
            pltpu.SemaphoreType.DMA((CHUNKS // 2,)),
        ],
        compiler_params=pltpu.CompilerParams(
            collective_id=1, has_side_effects=True, vmem_limit_bytes=40 * 2**20
        ),
        cost_estimate=pl.CostEstimate(
            flops=2 * rows * 4 * depth * n, bytes_accessed=60_000_000, transcendentals=0
        ),
        name="project",
    )(tokens, w)


def attention_kernel(
    ny,
    nz,
    packed_ref,
    do_ref,
    wo_ref,
    woth_ref,
    out_ref,
    dp_ref,
    q_all,
    kv_all,
    u_all,
    do_v,
    wo_v,
    ups,
    upr,
    s_all,
    o_snd,
    o_rcv,
    st_snd,
    st_rcv,
    ld_snd,
    ld_rcv,
    att_all,
    dq_acc,
    dq_snd,
    dq_rcv,
    dkv_own,
    dkv_snd,
    dkv_rcv,
    row_snd,
    row_rcv,
    dp_all,
    lsem,
    zs,
    zr,
    kvs,
    kvr,
    cs,
    cr,
    ds,
    dr,
    gs,
    gr,
):
    s, r, c = lax.axis_index("seq"), lax.axis_index("row"), lax.axis_index("col")
    y, z = s // nz, lax.rem(s, nz)
    factor = 1.0 / math.sqrt(HEAD)
    width = do_ref.shape[1]
    part = width // NJ
    sibling, across, far = flip(c, 1), flip(c, 2), flip(c, 3)
    cols = [sibling, across, far]
    slab = 2 * HEAD

    def at_z(d):
        return lax.rem(z + d + nz, nz)

    def dev_z(d):
        return (y * nz + at_z(d), r, c)

    def dev_y(yy):
        return (yy * nz + z, r, c)

    to_row = (s, 1 - r, c)
    to_cols = [(s, r, p) for p in cols]
    to_diag = (s, 1 - r, across)

    loads = [
        pltpu.make_async_copy(do_ref, do_v, lsem.at[0]),
        pltpu.make_async_copy(
            wo_ref.at[:, pl.ds(pl.multiple_of(c * width, 128), width)], wo_v.at[c], lsem.at[1]
        ),
    ]
    for j in range(NJ):
        for h, p in enumerate((across, far)):
            loads.append(
                pltpu.make_async_copy(
                    woth_ref.at[pl.ds(j * HEAD, HEAD), pl.ds(h * part, part)],
                    wo_v.at[p, :, pl.ds(j * part, part)],
                    lsem.at[2 + 2 * j + h],
                )
            )
    for load in loads:
        load.start()

    def z_rows(zz):
        return pl.ds(pl.multiple_of(zz * HEAD, HEAD), HEAD)

    def kv_rows(yy, rr):
        return pl.ds(pl.multiple_of(yy * slab + rr * HEAD, HEAD), HEAD)

    q_all[z_rows(z), :] = packed_ref[:, :HEAD]
    kv_all[kv_rows(y, r), :] = packed_ref[:, HEAD:]

    greet(
        [dev_z(d) for d in range(1, nz)]
        + [(lax.rem(y + d, ny) * nz + z, r, c) for d in range(1, ny)]
        + [to_row]
        + to_cols
        + [to_diag]
    )

    def kv_row():
        rows = kv_rows(y, r)
        return remote(kv_all.at[rows], kv_all.at[rows], kvs.at[0], kvr.at[2 * ny], to_row)

    def kv_row_arrival():
        rows = kv_rows(y, 1 - r)
        return remote(kv_all.at[rows], kv_all.at[rows], kvs.at[0], kvr.at[2 * ny], to_row)

    def kv_send(d, other):
        rr = 1 - r if other else r
        rows = kv_rows(y, rr)
        return remote(
            kv_all.at[rows],
            kv_all.at[rows],
            kvs.at[1 + 2 * d + other],
            kvr.at[2 * y + other],
            dev_y(lax.rem(y + d, ny)),
        )

    def kv_arrival(yy, other):
        rr = 1 - r if other else r
        rows = kv_rows(yy, rr)
        return remote(kv_all.at[rows], kv_all.at[rows], kvs.at[0], kvr.at[2 * yy + other], to_row)

    kv_row().start()
    for d in range(1, ny):

        @pl.when(y + d < ny)
        def _():
            kv_send(d, 0).start()

    def z_gather(kind, buf, d):
        return remote(buf.at[z_rows(z)], buf.at[z_rows(z)], zs.at[kind, d], zr.at[kind, d], dev_z(d))

    def z_gather_arrival(kind, buf, d):
        rows = z_rows(at_z(-d))
        return remote(buf.at[rows], buf.at[rows], zs.at[kind, d], zr.at[kind, d], dev_z(d))

    def z_give(kind, src, dst, d):
        return remote(src.at[at_z(d)], dst.at[z], zs.at[kind, d], zr.at[kind, d], dev_z(d))

    def z_give_arrival(kind, dst, d):
        slot = at_z(-d)
        return remote(dst.at[slot], dst.at[slot], zs.at[kind, d], zr.at[kind, d], dev_z(d))

    order = sorted(range(1, nz), key=lambda d: -min(d, nz - d))
    for d in order:
        z_gather(0, q_all, d).start()

    wo_sib = remote(
        wo_ref.at[:, pl.ds(pl.multiple_of(sibling * width, 128), width)],
        wo_v.at[c],
        cs.at[0, 0],
        cr.at[0, 0],
        to_cols[0],
    )
    wo_sib.start()
    wo_sib_in = remote(wo_v.at[sibling], wo_v.at[sibling], cs.at[0, 0], cr.at[0, 0], to_cols[0])

    kv_row_arrival().wait_recv()
    for d in range(1, ny):

        @pl.when(y + d < ny)
        def _():
            kv_send(d, 1).start()

    for load in loads:
        load.wait()
    wo_sib_in.wait_recv()
    ups_copies = []
    for h, p in enumerate(cols):
        ups[p] = dot_nt(do_v[...], wo_v[p])
        copy = remote(ups.at[p], upr.at[c], cs.at[1, h], cr.at[1, h], to_cols[h])
        copy.start()
        ups_copies.append(copy)
    upr[c] = dot_nt(do_v[...], wo_v[c])

    for d in order:
        z_gather_arrival(0, q_all, d).wait_recv()
    nq = nz * HEAD
    lane = lax.broadcasted_iota(jnp.int32, (1, nq), 1)
    qpos = (y * nz + lane // HEAD) * slab + r * HEAD + lane % HEAD
    kofs = lax.broadcasted_iota(jnp.int32, (slab, 1), 0)

    def y_rows(yy):
        return pl.ds(pl.multiple_of(yy * slab, slab), slab)

    def score_turn(yy, largest):
        @pl.when(yy < y)
        def _():
            kv_arrival(yy, 0).wait_recv()
            kv_arrival(yy, 1).wait_recv()

        keys = kv_all[y_rows(yy), :HEAD]
        scores = dot_nt(keys, q_all[...]) * factor
        kpos = (yy * nz + z) * slab + kofs
        scores = jnp.where(kpos <= qpos, scores, masked_score)
        s_all[y_rows(yy), :] = scores
        return jnp.maximum(largest, jnp.max(scores, axis=0, keepdims=True))

    largest = lax.fori_loop(0, y + 1, score_turn, jnp.full((1, nq), masked_score, F32))

    def weight_turn(yy, carry):
        total, mixed = carry
        weights = jnp.exp(s_all[y_rows(yy), :] - largest)
        total = total + jnp.sum(weights, axis=0, keepdims=True)
        mixed = mixed + dot_tn(kv_all[y_rows(yy), HEAD:], weights.astype(BF))
        return total, mixed

    total, mixed = lax.fori_loop(
        0, y + 1, weight_turn, (jnp.zeros((1, nq), F32), jnp.zeros((HEAD, nq), F32))
    )
    for zz in range(nz):
        lanes = slice(zz * HEAD, (zz + 1) * HEAD)
        o_snd[zz] = mixed[:, lanes].astype(BF)
        st_snd[zz, 0:1, :] = largest[:, lanes]
        st_snd[zz, 1:2, :] = total[:, lanes]
    for d in order:
        z_give(1, o_snd, o_rcv, d).start()
        z_give(2, st_snd, st_rcv, d).start()
    o_rcv[z] = o_snd[z]
    st_rcv[z] = st_snd[z]

    for h, p in enumerate(cols):
        remote(upr.at[p], upr.at[p], cs.at[1, h], cr.at[1, h], to_cols[h]).wait_recv()
    up = (upr[0] + upr[1] + upr[2] + upr[3]).astype(BF)
    u_all[z_rows(z), :] = up
    for d in order:
        z_gather(3, u_all, d).start()
    up_t = up.astype(F32).T

    for d in order:
        z_give_arrival(2, st_rcv, d).wait_recv()
        z_give_arrival(1, o_rcv, d).wait_recv()
    top = st_rcv[0, 0:1, :]
    for zz in range(1, nz):
        top = jnp.maximum(top, st_rcv[zz, 0:1, :])
    full_total = jnp.zeros((1, HEAD), F32)
    full = jnp.zeros((HEAD, HEAD), F32)
    for zz in range(nz):
        scale = jnp.exp(st_rcv[zz, 0:1, :] - top)
        full_total = full_total + scale * st_rcv[zz, 1:2, :]
        full = full + scale * o_rcv[zz].astype(F32)
    att_t = (full / full_total).astype(BF).astype(F32)
    ld_snd[0:1, :] = top + jnp.log(full_total)
    ld_snd[1:2, :] = jnp.sum(up_t * att_t, axis=0, keepdims=True)
    ld_rcv[z] = ld_snd[...]

    def ld_copy(d):
        return remote(ld_snd, ld_rcv.at[z], zs.at[4, d], zr.at[4, d], dev_z(d))

    for d in order:
        ld_copy(d).start()
    att_all[c] = att_t.T.astype(BF)
    att_copies = []
    for h, p in enumerate(cols):
        copy = remote(att_all.at[c], att_all.at[c], cs.at[2, h], cr.at[2, h], to_cols[h])
        copy.start()
        att_copies.append(copy)

    for d in order:
        z_gather_arrival(3, u_all, d).wait_recv()
        z_give_arrival(4, ld_rcv, d).wait_recv()
    logsum = jnp.concatenate([ld_rcv[zz, 0:1, :] for zz in range(nz)], axis=1)
    delta = jnp.concatenate([ld_rcv[zz, 1:2, :] for zz in range(nz)], axis=1)

    def dkv_send(yy):
        return remote(
            dkv_snd.at[y_rows(yy)], dkv_rcv.at[y_rows(y)], ds.at[yy], dr.at[y], dev_y(yy)
        )

    def grad_turn(yy, dq):
        keys, values = kv_all[y_rows(yy), :HEAD], kv_all[y_rows(yy), HEAD:]
        probs = jnp.exp(s_all[y_rows(yy), :] - logsum)
        prob_grad = dot_nt(values, u_all[...])
        score_grad = (probs * (prob_grad - delta)).astype(BF)
        dk = jnp.dot(score_grad, q_all[...], preferred_element_type=F32) * factor
        dv = jnp.dot(probs.astype(BF), u_all[...], preferred_element_type=F32)
        dkv_own[:, :HEAD] = dk
        dkv_own[:, HEAD:] = dv

        @pl.when(yy < y)
        def _():
            dkv_snd[y_rows(yy), :] = dkv_own[...].astype(BF)
            dkv_send(yy).start()

        return dq + dot_tn(keys, score_grad)

    dq = lax.fori_loop(0, y + 1, grad_turn, jnp.zeros((HEAD, nq), F32))
    for zz in range(nz):
        dq_snd[zz] = (dq[:, zz * HEAD : (zz + 1) * HEAD] * factor).astype(BF)
    for d in order:
        z_give(5, dq_snd, dq_rcv, d).start()

    for h, p in enumerate(cols):
        remote(att_all.at[p], att_all.at[p], cs.at[2, h], cr.at[2, h], to_cols[h]).wait_recv()
    for j in range(NJ):
        lanes = pl.ds(j * part, part)
        total_out = jnp.dot(att_all[0], wo_v[0, :, lanes], preferred_element_type=F32)
        for p in range(1, 4):
            total_out = total_out + jnp.dot(
                att_all[p], wo_v[p, :, lanes], preferred_element_type=F32
            )
        out_ref[:, lanes] = total_out.astype(BF)

    for d in range(1, ny):

        @pl.when(y + d < ny)
        def _():
            yy = lax.rem(y + d, ny)
            remote(
                dkv_rcv.at[y_rows(yy)], dkv_rcv.at[y_rows(yy)], ds.at[0], dr.at[yy], to_row
            ).wait_recv()
            dkv_own[...] += dkv_rcv[y_rows(yy), :].astype(F32)

    mine = pl.ds(pl.multiple_of(r * HEAD, HEAD), HEAD)
    theirs = pl.ds(pl.multiple_of((1 - r) * HEAD, HEAD), HEAD)
    row_snd[...] = dkv_own[theirs, :].astype(BF)
    row_copy = remote(row_snd, row_rcv, ds.at[ny], dr.at[ny], to_row)
    row_copy.start()
    dq_sum = dq_snd[z].astype(F32)
    for d in order:
        z_give_arrival(5, dq_rcv, d).wait_recv()
        dq_sum = dq_sum + dq_rcv[at_z(-d)].astype(F32)
    dp_all[c, mine, :HEAD] = dq_sum.T.astype(BF)
    row_copy.wait_recv()
    dp_all[c, mine, HEAD:] = (dkv_own[mine, :] + row_rcv[...].astype(F32)).astype(BF)

    peers = [(r, across), (1 - r, c), (1 - r, across)]

    def dp_rows(rr):
        return pl.ds(pl.multiple_of(rr * HEAD, HEAD), HEAD)

    def dp_copy(i):
        src = dp_all.at[c, mine]
        dev = to_cols[0] if i == 3 else (s,) + peers[i]
        return remote(src, src, gs.at[i], gr.at[i], dev)

    def dp_relay(i):
        rr, cc = peers[i]
        src = dp_all.at[cc, dp_rows(rr)]
        return remote(src, src, gs.at[4 + i], gr.at[4 + i], to_cols[0])

    def dp_arrival(i):
        if i == 3:
            rr, cc = r, sibling
        elif i < 3:
            rr, cc = peers[i]
        else:
            rr, cc = ((r, far), (1 - r, sibling), (1 - r, far))[i - 4]
        src = dp_all.at[cc, dp_rows(rr)]
        return remote(src, src, gs.at[i], gr.at[i], to_cols[0])

    for i in (2, 0, 1, 3):
        dp_copy(i).start()
    for i in (0, 1, 2):
        dp_arrival(i).wait_recv()
        dp_relay(i).start()
    for i in range(3, 7):
        dp_arrival(i).wait_recv()
    dp_ref[...] = dp_all[...]

    kv_row().wait_send()
    for d in range(1, ny):

        @pl.when(y + d < ny)
        def _():
            kv_send(d, 0).wait_send()
            kv_send(d, 1).wait_send()

    def sent_turn(yy, carry):
        dkv_send(yy).wait_send()
        return carry

    lax.fori_loop(0, y, sent_turn, 0)
    for d in order:
        z_gather(0, q_all, d).wait_send()
        z_give(1, o_snd, o_rcv, d).wait_send()
        z_give(2, st_snd, st_rcv, d).wait_send()
        z_gather(3, u_all, d).wait_send()
        ld_copy(d).wait_send()
        z_give(5, dq_snd, dq_rcv, d).wait_send()
    wo_sib.wait_send()
    row_copy.wait_send()
    for copy in ups_copies + att_copies:
        copy.wait_send()
    for i in range(4):
        dp_copy(i).wait_send()
    for i in range(3):
        dp_relay(i).wait_send()


def attention(ny, nz, packed, cotangent, wo, wo_other):
    width = cotangent.shape[1]
    hbm = pl.BlockSpec(memory_space=pl.ANY)
    vm = pl.BlockSpec(memory_space=pltpu.VMEM)
    nk, nq = ny * 2 * HEAD, nz * HEAD
    n = packed.shape[1]
    V = pltpu.VMEM
    sem = pltpu.SemaphoreType.DMA
    return pl.pallas_call(
        functools.partial(attention_kernel, ny, nz),
        out_shape=(
            jax.ShapeDtypeStruct(cotangent.shape, BF),
            jax.ShapeDtypeStruct((4, 2 * HEAD, n), BF),
        ),
        in_specs=[vm, hbm, hbm, hbm],
        out_specs=(vm, vm),
        scratch_shapes=[
            V((nq, HEAD), BF),
            V((nk, 2 * HEAD), BF),
            V((nq, HEAD), BF),
            V((HEAD, width), BF),
            V((4, HEAD, width), BF),
            V((4, HEAD, HEAD), F32),
            V((4, HEAD, HEAD), F32),
            V((nk, nq), F32),
            V((nz, HEAD, HEAD), BF),
            V((nz, HEAD, HEAD), BF),
            V((nz, 8, HEAD), F32),
            V((nz, 8, HEAD), F32),
            V((8, HEAD), F32),
            V((nz, 8, HEAD), F32),
            V((4, HEAD, HEAD), BF),
            V((HEAD, nq), F32),
            V((nz, HEAD, HEAD), BF),
            V((nz, HEAD, HEAD), BF),
            V((2 * HEAD, 2 * HEAD), F32),
            V((nk, 2 * HEAD), BF),
            V((nk, 2 * HEAD), BF),
            V((HEAD, 2 * HEAD), BF),
            V((HEAD, 2 * HEAD), BF),
            V((4, 2 * HEAD, n), BF),
            sem((2 + 2 * NJ,)),
            sem((6, nz)),
            sem((6, nz)),
            sem((1 + 2 * ny + 2,)),
            sem((2 * ny + 1,)),
            sem((3, 3)),
            sem((3, 3)),
            sem((ny + 1,)),
            sem((ny + 1,)),
            sem((7,)),
            sem((7,)),
        ],
        compiler_params=pltpu.CompilerParams(
            collective_id=2, has_side_effects=True, vmem_limit_bytes=48 * 2**20
        ),
        cost_estimate=pl.CostEstimate(
            flops=3_000_000_000, bytes_accessed=120_000_000, transcendentals=2_000_000
        ),
        name="attention",
    )(packed, cotangent, wo, wo_other)


def input_grad_kernel(c_ref, dp_ref, own_ref, sib_ref, oth_ref, out_ref):
    c = c_ref[0]
    n = own_ref.shape[1]
    acc = dot_nt(dp_ref[c], own_ref[...])
    acc = acc + dot_nt(dp_ref[flip(c, 1)], sib_ref[...])
    acc = acc + dot_nt(dp_ref[flip(c, 2)], oth_ref[:, :n])
    acc = acc + dot_nt(dp_ref[flip(c, 3)], oth_ref[:, n:])
    out_ref[...] = acc.astype(BF)


def input_grad(dp, w, w_sib, w_other):
    depth, n = w_sib.shape
    rows = dp.shape[1]
    blk = min(256, depth)
    steps = depth // blk
    c = lax.axis_index("col").astype(jnp.int32).reshape(1)
    return pl.pallas_call(
        input_grad_kernel,
        out_shape=jax.ShapeDtypeStruct((rows, depth), BF),
        grid_spec=pltpu.PrefetchScalarGridSpec(
            num_scalar_prefetch=1,
            grid=(steps,),
            in_specs=[
                pl.BlockSpec(dp.shape, lambda i, c: (0, 0, 0)),
                pl.BlockSpec((blk, n), lambda i, c: (c[0] * steps + i, 0)),
                pl.BlockSpec((blk, n), lambda i, c: (i, 0)),
                pl.BlockSpec((blk, 2 * n), lambda i, c: (i, 0)),
            ],
            out_specs=pl.BlockSpec((rows, blk), lambda i, c: (0, i)),
        ),
        name="input_grad",
    )(c, dp, w, w_sib, w_other)


def body(nz, tokens, input_weight, output_weight, output_cotangent):
    ny = lax.axis_size("seq") // nz
    seed_w, seed_wo = seeds(input_weight, output_weight)
    wo_other = lax.all_gather(seed_wo, "seq", axis=0, tiled=True)
    w_other = lax.all_gather(seed_w, "seq", axis=0, tiled=True)
    packed, w_sib = project(tokens, input_weight)
    layer_output, dp = attention(
        ny, nz, packed, output_cotangent, output_weight, wo_other
    )
    return layer_output, input_grad(dp, input_weight, w_sib, w_other)


def solution(mesh):
    nz = 8 if mesh.shape["seq"] % 32 == 0 else 2
    return jax.shard_map(
        functools.partial(body, nz),
        mesh=mesh,
        in_specs=(
            P("seq", ("row", "col")),
            P("row", "col"),
            P("col", None),
            P(("seq", "row"), "col"),
        ),
        out_specs=(P(("seq", "row"), "col"), P("seq", ("row", "col"))),
        check_vma=False,
    )
```

time: 1140 us -> 189 us (0.17)
  starting transfers between devices: 441 us -> 0.08 us
  waiting for transfers between devices: 337 us -> 67.6 us
  matrix products: 235 us -> 0 us
  Pallas kernels: 0 us -> 97.3 us
  local copies, waits for them, and re-layouts: 50 us -> 6.51 us
  other arithmetic: 38.8 us -> 0 us
    ppermute x95 -> x0, starting transfers between devices: 440 us -> none  [the longest x63 317 us: shifted(): return lax.ppermute(block, axis, route)]
    dot_general x232 -> x0, matrix products: 235 us -> none  [the longest x33 52.2 us: gradient_block(): jnp.einsum('hqk,hkd->hqd', score_grad, key_values[0], preferred_element_t...]
    reduce_scatter x4 -> x0, waiting for transfers between devices: 209 us -> none  [the longest x1 71.2 us: body(): key_sums = lax.psum_scatter(key_acc, 'row', scatter_dimension=2, tiled=True)]
    pallas_call x0 -> x4, Pallas kernels: none -> 97.3 us  [the longest x1 55.2 us: attention(): pl.pallas_call(functools.partial(attention_kernel, ny, nz), out_shape=(ja...]
    ppermute x95 -> x0, waiting for transfers between devices: 79.6 us -> none  [the longest x63 73.5 us: shifted(): return lax.ppermute(block, axis, route)]
    while x97 -> x0, local copies, waits for them, and re-layouts: 43.9 us -> none
    add x130 -> x0, other arithmetic: 24.1 us -> none  [the longest x32 23.4 us: key_turn(): return (key_values, key_acc + more_keys, query_grad + more_grad)]
    all_gather x2, waiting for transfers between devices: 46.5 us -> 66.9 us  [the longest x1 43.5 us: body(): wo_other = lax.all_gather(seed_wo, 'seq', axis=0, tiled=True)]
  transfers between devices with their start and end apart: 101 -> 2, of which waited for: 60 -> 2; matrix products, arithmetic and copies ran while one was open for 25% -> 0% of each run, Pallas kernels for 0% -> 44%
where the time goes in v1:
time: 189 us; the launch traced here: 186 us
  Pallas kernels  97.3 us (51%)
  waiting for transfers between devices  67.6 us (36%)
  between operations  14.1 us (7%)
  local copies, waits for them, and re-layouts  6.51 us (3%)
    pallas_call x1, Pallas kernels, attention(): pl.pallas_call(functools.partial(attention_kernel, ny, nz), out_shape=(ja...  55.2 us
    all_gather x1, waiting for transfers between devices, body(): wo_other = lax.all_gather(seed_wo, 'seq', axis=0, tiled=True)  43.5 us
    pallas_call x1, Pallas kernels, project(): pl.pallas_call(proj_kernel, out_shape=(jax.ShapeDtypeStruct((half, n), BF...  26.2 us
    all_gather x1, waiting for transfers between devices, body(): w_other = lax.all_gather(seed_w, 'seq', axis=0, tiled=True)  23.4 us
    pallas_call x1, Pallas kernels, seeds(): pl.pallas_call(functools.partial(seed_kernel, ns), out_shape=(jax.ShapeDt...  9.32 us
    pallas_call x1, Pallas kernels, input_grad(): pl.pallas_call(input_grad_kernel, out_shape=jax.ShapeDtypeStruct((rows, d...  6.59 us
    unnamed x13, local copies, waits for them, and re-layouts  6.51 us
  transfers between devices with their start and end apart: 2, of which 2 were waited for; matrix products, arithmetic and copies ran while one was open for 0% of the time, Pallas kernels for 44%

profile of v1, /device:TPU:1, one launch (start us, length us, event | category | flops | bytes accessed | tf_op | source)
XLA Modules:
  0.0 185.6 jit_solution(483793225070416207)
XLA Ops:
  7.2 0.0 copy-start.3
  7.2 0.0 all-gather.3.cloned.1.call-start
  7.2 9.3 %seeds.1 = (bf16[48,768]{1,0:T(8,128)(2,1)}, bf16[16,1536]{1,0:T(8,128)(2,1)}) custom-call(bf16[6144,384]{1,0:T(8,128)(2,1)} %own_ref.1, bf16[128,12288]{1,0:T(8,128)(2,1)} %wo_ref.3), custom_call_target="tpu_custom_call" | custom-call | tf_op jit(solution)/shard_map/seeds/pallas_call | solution.py:104
  16.5 0.0 all-gather.3.cloned.1.call-update
  16.6 0.0 all-gather.5.cloned.1.call-start
  16.6 0.7 all-gather.5.cloned.1.call-update
  17.3 0.0 copy-done.3
  17.3 0.0 copy-start
  17.3 2.3 %copy-done = bf16[6144,384]{1,0:T(8,128)(2,1)S(1)} copy-done((bf16[6144,384]{1,0:T(8,128)(2,1)S(1)}, bf16[6144,384]{1,0:T(8,128)(2,1)}, u32[]{:S(2)}) %copy-start) | copy-done | bytes 4718616
  19.7 0.0 copy-start.5
  19.7 26.2 %project.1 = (bf16[128,384]{1,0:T(8,128)(2,1)S(1)}, bf16[1536,384]{1,0:T(8,128)(2,1)S(1)}) custom-call(bf16[256,1536]{1,0:T(8,128)(2,1)S(1)} %copy-done.3, bf16[6144,384]{1,0:T(8,128)(2,1)S(1)} %copy-done), custom_call_target="tpu_custom_call" | custom-call | flops 1207959552 | bytes 60000000 | tf_op jit(solution)/shard_map/project/pallas_call | solution.py:219
  45.9 0.0 copy-start.1
  45.9 1.0 copy-done.1
  46.9 43.5 %all-gather.3.cloned.1.call-done.woth_ref = bf16[512,1536]{1,0:T(8,128)(2,1)} async-done(((bf16[16,1536]{1,0:T(8,128)(2,1)}), bf16[512,1536]{1,0:T(8,128)(2,1)}) %all-gather.3.cloned.1.call-update) | async-done | bytes 1572880 | tf_op jit(solution)/shard_map/all_gather | solution.py:744
  90.4 0.0 copy-done.5
  90.4 0.0 copy-start.4
  90.4 1.4 copy-done.4
  91.8 55.2 %attention.1 = (bf16[128,3072]{1,0:T(8,128)(2,1)S(1)}, bf16[4,256,384]{2,1,0:T(8,128)(2,1)S(1)}) custom-call(bf16[128,384]{1,0:T(8,128)(2,1)S(1)} %get-tuple-element.8.packed_ref, bf16[128,3072]{1,0:T(8,128)(2,1)S(1)} %copy-done.5, bf16[128,12288]{1,0:T(8,128)(2,1)} %wo_ref.3, bf16[512,1536]{1,0:T(8,128)(2,1)S(1)} %copy-done.4), custom_call_target="tpu_custom_call" | custom-call | flops 3000000000 | bytes 120000000 | tf_op jit(solution)/shard_map/attention/pallas_call | solution.py:652
  147.0 0.0 copy-start.2
  147.0 0.9 copy-done.2
  147.9 23.4 %all-gather.5.cloned.1.call-done.oth_ref = bf16[1536,768]{1,0:T(8,128)(2,1)} async-done(((bf16[48,768]{1,0:T(8,128)(2,1)}), bf16[1536,768]{1,0:T(8,128)(2,1)}) %all-gather.5.cloned.1.call-update) | async-done | bytes 2359312 | tf_op jit(solution)/shard_map/all_gather | solution.py:745
  171.3 6.6 %input_grad.1 = bf16[256,1536]{1,0:T(8,128)(2,1)} custom-call(s32[1]{0:T(128)} %bitcast.c_ref, bf16[4,256,384]{2,1,0:T(8,128)(2,1)} %copy-done.2, bf16[6144,384]{1,0:T(8,128)(2,1)} %own_ref.1, bf16[1536,384]{1,0:T(8,128)(2,1)} %copy-done.1, bf16[1536,768]{1,0:T(8,128)(2,1)} %all-gather.5.cloned.1.call-done.oth_ref), custom_call_target="tpu_custom_call" | custom-call | tf_op jit(solution)/shard_map/input_grad/pallas_call | solution.py:723
  177.9 0.9 copy.7
Async XLA Ops:
  7.2 10.2 %copy-start.3 = (bf16[256,1536]{1,0:T(8,128)(2,1)S(1)}, bf16[256,1536]{1,0:T(8,128)(2,1)}, u32[]{:S(2)}) copy-start(bf16[256,1536]{1,0:T(8,128)(2,1)} %t_ref.1) | copy-start | bytes 2359300
  7.2 83.2 %all-gather.3.cloned.1.call-start = ((), (), s32[]{:S(2)}) async-start(), calls=%async_computation | async-start | bytes 1622016 | tf_op jit(solution)/shard_map/all_gather | solution.py:744
  16.6 154.7 %all-gather.5.cloned.1.call-start = ((), (), s32[]{:S(2)}) async-start(), calls=%async_computation.1 | async-start | bytes 2433024 | tf_op jit(solution)/shard_map/all_gather | solution.py:745
  17.3 2.3 %copy-start = (bf16[6144,384]{1,0:T(8,128)(2,1)S(1)}, bf16[6144,384]{1,0:T(8,128)(2,1)}, u32[]{:S(2)}) copy-start(bf16[6144,384]{1,0:T(8,128)(2,1)} %own_ref.1) | copy-start | bytes 14155780
  19.7 70.7 %copy-start.5 = (bf16[128,3072]{1,0:T(8,128)(2,1)S(1)}, bf16[128,3072]{1,0:T(8,128)(2,1)}, u32[]{:S(2)}) copy-start(bf16[128,3072]{1,0:T(8,128)(2,1)} %do_ref.1) | copy-start | bytes 2359300
  45.9 1.0 copy-start.1
  90.4 1.4 copy-start.4
  147.0 0.9 copy-start.2
Sparse Core Ops, SparseCore 0:
  16.7 73.6 all-gather.2
  93.0 78.2 all-gather.4

commit v2 on v1

v2 whole, which is shorter than its diff:
```python
import functools
import math

import jax
import jax.numpy as jnp
from jax import lax
from jax.experimental import pallas as pl
from jax.experimental.pallas import tpu as pltpu
from jax.sharding import PartitionSpec as P

HEAD = 128
MESH = pl.DeviceIdType.MESH
masked_score = -1e30
BF = jnp.bfloat16
F32 = jnp.float32
CHUNKS = 4


def remote(src, dst, send_sem, recv_sem, device):
    return pltpu.make_async_remote_copy(
        src_ref=src,
        dst_ref=dst,
        send_sem=send_sem,
        recv_sem=recv_sem,
        device_id=device,
        device_id_type=MESH,
    )


def greet(devices):
    barrier = pltpu.get_barrier_semaphore()
    for device in devices:
        pl.semaphore_signal(barrier, inc=1, device_id=device, device_id_type=MESH)
    pl.semaphore_wait(barrier, len(devices))


def dot_nt(a, b):
    return lax.dot_general(a, b, (((1,), (1,)), ((), ())), preferred_element_type=F32)


def dot_tn(a, b):
    return lax.dot_general(a, b, (((0,), (0,)), ((), ())), preferred_element_type=F32)


def flip(c, bits):
    low, high = lax.rem(c, 2), c // 2
    if bits & 1:
        low = 1 - low
    if bits & 2:
        high = 1 - high
    return high * 2 + low


def ring(size):
    return size // 2, (size - 1) // 2


def layer_kernel(
    ny,
    nz,
    t_ref,
    w_ref,
    wo_ref,
    do_ref,
    out_ref,
    dx_ref,
    tbuf,
    wv,
    psend,
    precv,
    w_x,
    wo_v,
    q_all,
    kv_all,
    u_all,
    do_v,
    ups,
    upr,
    s_all,
    o_snd,
    o_rcv,
    st_snd,
    st_rcv,
    ld_snd,
    ld_rcv,
    att_all,
    dq_snd,
    dq_rcv,
    dkv_own,
    dkv_snd,
    dkv_rcv,
    row_snd,
    row_rcv,
    dp_all,
    lsem,
    sds,
    sdr,
    wzs,
    wzr,
    wys,
    wyr,
    oys,
    oyr,
    ozs,
    ozr,
    sbs,
    sbr,
    tks,
    tkr,
    pts,
    ptr,
    zs,
    zr,
    kvs,
    kvr,
    cs,
    cr,
    ds,
    dr,
    gs,
    gr,
):
    s, r, c = lax.axis_index("seq"), lax.axis_index("row"), lax.axis_index("col")
    y, z = s // nz, lax.rem(s, nz)
    core = lax.rem(c, 2)
    sgn = 1 - 2 * core
    factor = 1.0 / math.sqrt(HEAD)
    depth = t_ref.shape[1]
    width = do_ref.shape[1]
    step = 2 * HEAD // CHUNKS
    hk = CHUNKS // 2
    slab = 2 * HEAD
    cols = [c, flip(c, 1), flip(c, 2), flip(c, 3)]
    to_cols = [(s, r, p) for p in cols]
    to_row = (s, 1 - r, c)
    to_diag = (s, 1 - r, cols[2])

    def wrap(a, n):
        return lax.rem(a + 2 * n, n)

    def dev_z(zz):
        return (y * nz + zz, r, c)

    def dev_y(yy):
        return (yy * nz + z, r, c)

    own_tokens = pltpu.make_async_copy(t_ref, tbuf.at[0], lsem.at[0])
    own_w = pltpu.make_async_copy(w_ref, wv, lsem.at[1])
    own_wo = pltpu.make_async_copy(
        wo_ref.at[:, pl.ds(pl.multiple_of(c * width, 128), width)], wo_v.at[0], lsem.at[2]
    )
    own_do = pltpu.make_async_copy(do_ref, do_v, lsem.at[3])
    own_tokens.start()
    own_w.start()
    own_wo.start()
    own_do.start()
    greet(
        [dev_z(wrap(z + d, nz)) for d in range(1, nz)]
        + [dev_y(wrap(y + d, ny)) for d in range(1, ny)]
        + [to_row]
        + to_cols[1:]
        + [to_diag]
    )

    piece = depth // (ny * nz)
    orow = HEAD // nz
    part = width // ny

    def w_piece(yy, zz):
        start = pl.multiple_of((yy * nz + zz) * piece, 16)
        return w_x.at[pl.ds(1, 2), pl.ds(start, piece), :]

    def o_piece(yy, zz):
        return wo_v.at[
            pl.ds(2, 2),
            pl.ds(pl.multiple_of(zz * orow, 16), orow),
            pl.ds(pl.multiple_of(yy * part, 128), part),
        ]

    def o_super(zz):
        return wo_v.at[pl.ds(2, 2), pl.ds(pl.multiple_of(zz * orow, 16), orow), :]

    seeds = []
    for h in range(2):
        p = cols[2 + h]
        start = pl.multiple_of(s * piece, 16)
        seeds.append(
            remote(
                w_ref.at[pl.ds(pl.multiple_of(p * depth + s * piece, 16), piece), :],
                w_x.at[1 + h, pl.ds(start, piece), :],
                sds.at[0, h],
                sdr.at[0, h],
                to_cols[2 + h],
            )
        )
        orows = pl.ds(pl.multiple_of(z * orow, 16), orow)
        seeds.append(
            remote(
                wo_ref.at[orows, pl.ds(pl.multiple_of(p * width + y * part, 128), part)],
                wo_v.at[2 + h, orows, pl.ds(pl.multiple_of(y * part, 128), part)],
                sds.at[1, h],
                sdr.at[1, h],
                to_cols[2 + h],
            )
        )
    for copy in seeds:
        copy.start()

    def rows_of(k):
        start = (1 - r) * HEAD + k * step if k < hk else r * HEAD + (k - hk) * step
        return pl.ds(pl.multiple_of(start, step), step)

    def token_copy(kind, k):
        rows = rows_of(k)
        if kind == 0:
            return remote(
                t_ref.at[rows], tbuf.at[2, rows], tks.at[0, k], tkr.at[0, k], to_cols[2]
            )
        if kind == 1:
            return remote(
                t_ref.at[rows], tbuf.at[1, rows], tks.at[1, k], tkr.at[1, k], to_cols[1]
            )
        return remote(
            tbuf.at[2, rows], tbuf.at[3, rows], tks.at[2, k], tkr.at[2, k], to_cols[1]
        )

    for k in range(CHUNKS):
        token_copy(0, k).start()
        token_copy(1, k).start()

    sib_w = remote(
        w_ref.at[pl.ds(pl.multiple_of(cols[1] * depth, 16), depth), :],
        w_x.at[0],
        sbs.at[0],
        sbr.at[0],
        to_cols[1],
    )
    sib_wo = remote(
        wo_ref.at[:, pl.ds(pl.multiple_of(cols[1] * width, 128), width)],
        wo_v.at[1],
        sbs.at[1],
        sbr.at[1],
        to_cols[1],
    )
    sib_wo.start()
    sib_w.start()

    zl, zsh = ring(nz)
    yl, ysh = ring(ny)
    z_next, z_prev = wrap(z + sgn, nz), wrap(z - sgn, nz)
    y_next, y_prev = wrap(y + sgn, ny), wrap(y - sgn, ny)

    def zq(long, t):
        return wrap(z - sgn * t, nz) if long else wrap(z + sgn * t, nz)

    def yq(long, t):
        return wrap(y - sgn * t, ny) if long else wrap(y + sgn * t, ny)

    def z_ring(pick, snd, rcv, long, t):
        ref = pick(zq(long, t))
        way = 0 if long else 1
        return remote(
            ref, ref, snd.at[way, t], rcv.at[way, t + 1], dev_z(z_next if long else z_prev)
        )

    def z_ring_in(pick, snd, rcv, long, t):
        ref = pick(zq(long, t))
        way = 0 if long else 1
        return remote(ref, ref, snd.at[way, t], rcv.at[way, t], dev_z(z_next))

    def y_ring(pick, snd, rcv, long, t):
        ref = pick(yq(long, t))
        way = 0 if long else 1
        return remote(
            ref, ref, snd.at[way, t], rcv.at[way, t + 1], dev_y(y_next if long else y_prev)
        )

    def y_ring_in(pick, snd, rcv, long, t):
        ref = pick(yq(long, t))
        way = 0 if long else 1
        return remote(ref, ref, snd.at[way, t], rcv.at[way, t], dev_y(y_next))

    started = []

    def go(copy):
        copy.start()
        started.append(copy)

    def w_here(zz):
        return w_piece(y, zz)

    def o_here(yy):
        return o_piece(yy, z)

    def z_start(pick, snd, rcv):
        if zl:
            go(z_ring(pick, snd, rcv, True, 0))
        if zsh:
            go(z_ring(pick, snd, rcv, False, 0))

    def y_start(pick, snd, rcv):
        if yl:
            go(y_ring(pick, snd, rcv, True, 0))
        if ysh:
            go(y_ring(pick, snd, rcv, False, 0))

    def z_round(pick, snd, rcv, t):
        ways = []
        for long, hops in ((True, zl), (False, zsh)):
            if t <= hops:
                z_ring_in(pick, snd, rcv, long, t).wait_recv()
                if t < hops:
                    go(z_ring(pick, snd, rcv, long, t))
                ways.append(long)
        return ways

    def y_round(pick, snd, rcv, t):
        for long, hops in ((True, yl), (False, ysh)):
            if t <= hops:
                y_ring_in(pick, snd, rcv, long, t).wait_recv()
                if t < hops:
                    go(y_ring(pick, snd, rcv, long, t))

    def w_column(long, t):
        zz = zq(long, t)
        index = t if long else zl + t

        def pick(yy):
            return w_piece(yy, zz)

        return pick, wys.at[index], wyr.at[index]

    def product(i, rows, start):
        return jnp.dot(
            tbuf[i, rows, :],
            wv[pl.ds(pl.multiple_of(start, 16), depth), :],
            preferred_element_type=F32,
        )

    def part_copy(k):
        rows = pl.ds(k * step, step)
        return remote(psend.at[rows], precv.at[rows], pts.at[k], ptr.at[k], to_row)

    def z_rows(zz):
        return pl.ds(pl.multiple_of(zz * HEAD, HEAD), HEAD)

    def kv_rows(yy, rr):
        return pl.ds(pl.multiple_of(yy * slab + rr * HEAD, HEAD), HEAD)

    def project(k):
        rows = rows_of(k)

        def arrived(kind):
            ref = tbuf.at[(2, 1, 3)[kind], rows]
            remote(ref, ref, tks.at[kind, k], tkr.at[kind, k], to_cols[1]).wait_recv()

        arrived(0)
        go(token_copy(2, k))
        arrived(1)
        acc = product(0, rows, c * depth) + product(1, rows, cols[1] * depth)
        acc = acc + product(2, rows, cols[2] * depth)
        arrived(2)
        acc = acc + product(3, rows, cols[3] * depth)
        if k < hk:
            psend[pl.ds(k * step, step), :] = acc
            go(part_copy(k))
        else:
            part_copy(k - hk).wait_recv()
            out = pl.ds((k - hk) * step, step)
            packed = (acc + precv[out, :]).astype(BF)
            q_all[pl.ds(pl.multiple_of(z * HEAD + (k - hk) * step, step), step), :] = packed[
                :, :HEAD
            ]
            start = pl.multiple_of(y * slab + r * HEAD + (k - hk) * step, step)
            kv_all[pl.ds(start, step), :] = packed[:, HEAD:]

    for copy in seeds:
        copy.wait_recv()
    z_start(w_here, wzs, wzr)
    y_start(o_here, oys, oyr)
    pick, snd, rcv = w_column(True, 0)
    y_start(pick, snd, rcv)
    columns = [[(True, 0)]]
    own_tokens.wait()
    own_w.wait()
    for t in range(1, yl + 1):
        y_round(o_here, oys, oyr, t)
    z_start(o_super, ozs, ozr)
    for k in range(max(CHUNKS, zl)):
        t = k + 1
        if k < CHUNKS:
            project(k)
        if t <= zl:
            ways = z_round(w_here, wzs, wzr, t)
            for long in ways:
                y_start(*w_column(long, t))
            columns.append([(long, t) for long in ways])
            for column in columns[t - 1]:
                y_round(*w_column(*column), 1)
            z_round(o_super, ozs, ozr, t)

    def kv_row():
        rows = kv_rows(y, r)
        return remote(kv_all.at[rows], kv_all.at[rows], kvs.at[0], kvr.at[2 * ny], to_row)

    def kv_row_arrival():
        rows = kv_rows(y, 1 - r)
        return remote(kv_all.at[rows], kv_all.at[rows], kvs.at[0], kvr.at[2 * ny], to_row)

    def kv_send(d, other):
        rr = 1 - r if other else r
        rows = kv_rows(y, rr)
        return remote(
            kv_all.at[rows],
            kv_all.at[rows],
            kvs.at[1 + 2 * d + other],
            kvr.at[2 * y + other],
            dev_y(wrap(y + d, ny)),
        )

    def kv_arrival(yy, other):
        rr = 1 - r if other else r
        rows = kv_rows(yy, rr)
        return remote(kv_all.at[rows], kv_all.at[rows], kvs.at[0], kvr.at[2 * yy + other], to_row)

    go(kv_row())
    for d in range(1, ny):

        @pl.when(y + d < ny)
        def _():
            kv_send(d, 0).start()

    def z_gather(kind, buf, d):
        return remote(
            buf.at[z_rows(z)],
            buf.at[z_rows(z)],
            zs.at[kind, d],
            zr.at[kind, d],
            dev_z(wrap(z + d, nz)),
        )

    def z_gather_arrival(kind, buf, d):
        rows = z_rows(wrap(z - d, nz))
        return remote(buf.at[rows], buf.at[rows], zs.at[kind, d], zr.at[kind, d], dev_z(z_next))

    def z_give(kind, src, dst, d):
        to = wrap(z + d, nz)
        return remote(src.at[to], dst.at[z], zs.at[kind, d], zr.at[kind, d], dev_z(to))

    def z_give_arrival(kind, dst, d):
        slot = wrap(z - d, nz)
        return remote(dst.at[slot], dst.at[slot], zs.at[kind, d], zr.at[kind, d], dev_z(z_next))

    order = sorted(range(1, nz), key=lambda d: -min(d, nz - d))
    for d in order:
        go(z_gather(0, q_all, d))

    for column in columns[zl]:
        y_round(*w_column(*column), 1)

    kv_row_arrival().wait_recv()
    for d in range(1, ny):

        @pl.when(y + d < ny)
        def _():
            kv_send(d, 1).start()

    own_do.wait()
    own_wo.wait()
    sib_wo.wait_recv()
    for i in range(1, 4):
        ups[i] = dot_nt(do_v[...], wo_v[i])
        go(remote(ups.at[i], upr.at[i], cs.at[0, i], cr.at[0, i], to_cols[i]))
    upr[0] = dot_nt(do_v[...], wo_v[0])

    for d in order:
        z_gather_arrival(0, q_all, d).wait_recv()
    nq = nz * HEAD
    lane = lax.broadcasted_iota(jnp.int32, (1, nq), 1)
    qpos = (y * nz + lane // HEAD) * slab + r * HEAD + lane % HEAD
    kofs = lax.broadcasted_iota(jnp.int32, (slab, 1), 0)

    def y_rows(yy):
        return pl.ds(pl.multiple_of(yy * slab, slab), slab)

    def score_turn(yy, largest):
        @pl.when(yy < y)
        def _():
            kv_arrival(yy, 0).wait_recv()
            kv_arrival(yy, 1).wait_recv()

        keys = kv_all[y_rows(yy), :HEAD]
        scores = dot_nt(keys, q_all[...]) * factor
        kpos = (yy * nz + z) * slab + kofs
        scores = jnp.where(kpos <= qpos, scores, masked_score)
        s_all[y_rows(yy), :] = scores
        return jnp.maximum(largest, jnp.max(scores, axis=0, keepdims=True))

    largest = lax.fori_loop(0, y + 1, score_turn, jnp.full((1, nq), masked_score, F32))

    def weight_turn(yy, carry):
        total, mixed = carry
        weights = jnp.exp(s_all[y_rows(yy), :] - largest)
        total = total + jnp.sum(weights, axis=0, keepdims=True)
        mixed = mixed + dot_tn(kv_all[y_rows(yy), HEAD:], weights.astype(BF))
        return total, mixed

    total, mixed = lax.fori_loop(
        0, y + 1, weight_turn, (jnp.zeros((1, nq), F32), jnp.zeros((HEAD, nq), F32))
    )
    for zz in range(nz):
        lanes = slice(zz * HEAD, (zz + 1) * HEAD)
        o_snd[zz] = mixed[:, lanes].astype(BF)
        st_snd[zz, 0:1, :] = largest[:, lanes]
        st_snd[zz, 1:2, :] = total[:, lanes]
    for d in order:
        go(z_give(1, o_snd, o_rcv, d))
        go(z_give(2, st_snd, st_rcv, d))
    o_rcv[z] = o_snd[z]
    st_rcv[z] = st_snd[z]

    for i in range(1, 4):
        remote(upr.at[i], upr.at[i], cs.at[0, i], cr.at[0, i], to_cols[i]).wait_recv()
    up = (upr[0] + upr[1] + upr[2] + upr[3]).astype(BF)
    u_all[z_rows(z), :] = up
    for d in order:
        go(z_gather(3, u_all, d))
    up_t = up.astype(F32).T

    for d in order:
        z_give_arrival(2, st_rcv, d).wait_recv()
        z_give_arrival(1, o_rcv, d).wait_recv()
    top = st_rcv[0, 0:1, :]
    for zz in range(1, nz):
        top = jnp.maximum(top, st_rcv[zz, 0:1, :])
    full_total = jnp.zeros((1, HEAD), F32)
    full = jnp.zeros((HEAD, HEAD), F32)
    for zz in range(nz):
        scale = jnp.exp(st_rcv[zz, 0:1, :] - top)
        full_total = full_total + scale * st_rcv[zz, 1:2, :]
        full = full + scale * o_rcv[zz].astype(F32)
    att_t = (full / full_total).astype(BF).astype(F32)
    ld_snd[0:1, :] = top + jnp.log(full_total)
    ld_snd[1:2, :] = jnp.sum(up_t * att_t, axis=0, keepdims=True)
    ld_rcv[z] = ld_snd[...]
    for d in order:
        go(remote(ld_snd, ld_rcv.at[z], zs.at[4, d], zr.at[4, d], dev_z(wrap(z + d, nz))))
    att_all[0] = att_t.T.astype(BF)
    for i in range(1, 4):
        go(remote(att_all.at[0], att_all.at[i], cs.at[1, i], cr.at[1, i], to_cols[i]))

    for d in order:
        z_gather_arrival(3, u_all, d).wait_recv()
        z_give_arrival(4, ld_rcv, d).wait_recv()
    logsum = jnp.concatenate([ld_rcv[zz, 0:1, :] for zz in range(nz)], axis=1)
    delta = jnp.concatenate([ld_rcv[zz, 1:2, :] for zz in range(nz)], axis=1)

    def dkv_send(yy):
        return remote(
            dkv_snd.at[y_rows(yy)], dkv_rcv.at[y_rows(y)], ds.at[yy], dr.at[y], dev_y(yy)
        )

    def grad_turn(yy, dq):
        keys, values = kv_all[y_rows(yy), :HEAD], kv_all[y_rows(yy), HEAD:]
        probs = jnp.exp(s_all[y_rows(yy), :] - logsum)
        prob_grad = dot_nt(values, u_all[...])
        score_grad = (probs * (prob_grad - delta)).astype(BF)
        dk = jnp.dot(score_grad, q_all[...], preferred_element_type=F32) * factor
        dv = jnp.dot(probs.astype(BF), u_all[...], preferred_element_type=F32)
        dkv_own[:, :HEAD] = dk
        dkv_own[:, HEAD:] = dv

        @pl.when(yy < y)
        def _():
            dkv_snd[y_rows(yy), :] = dkv_own[...].astype(BF)
            dkv_send(yy).start()

        return dq + dot_tn(keys, score_grad)

    dq = lax.fori_loop(0, y + 1, grad_turn, jnp.zeros((HEAD, nq), F32))
    for zz in range(nz):
        dq_snd[zz] = (dq[:, zz * HEAD : (zz + 1) * HEAD] * factor).astype(BF)
    for d in order:
        go(z_give(5, dq_snd, dq_rcv, d))

    for i in range(1, 4):
        remote(att_all.at[i], att_all.at[i], cs.at[1, i], cr.at[1, i], to_cols[i]).wait_recv()
    for j in range(ny):
        lanes = pl.ds(j * part, part)
        total_out = jnp.dot(att_all[0], wo_v[0, :, lanes], preferred_element_type=F32)
        for i in range(1, 4):
            total_out = total_out + jnp.dot(
                att_all[i], wo_v[i, :, lanes], preferred_element_type=F32
            )
        out_ref[:, lanes] = total_out.astype(BF)

    for d in range(1, ny):

        @pl.when(y + d < ny)
        def _():
            yy = wrap(y + d, ny)
            ref = dkv_rcv.at[y_rows(yy)]
            remote(ref, ref, ds.at[0], dr.at[yy], to_row).wait_recv()
            dkv_own[...] += dkv_rcv[y_rows(yy), :].astype(F32)

    def dp_rows(rr):
        return pl.ds(pl.multiple_of(rr * HEAD, HEAD), HEAD)

    mine, theirs = dp_rows(r), dp_rows(1 - r)
    row_snd[...] = dkv_own[theirs, :].astype(BF)
    row_copy = remote(row_snd, row_rcv, ds.at[ny], dr.at[ny], to_row)
    go(row_copy)
    dq_sum = dq_snd[z].astype(F32)
    for d in order:
        z_give_arrival(5, dq_rcv, d).wait_recv()
        dq_sum = dq_sum + dq_rcv[wrap(z - d, nz)].astype(F32)
    dp_all[0, mine, :HEAD] = dq_sum.T.astype(BF)
    row_copy.wait_recv()
    dp_all[0, mine, HEAD:] = (dkv_own[mine, :] + row_rcv[...].astype(F32)).astype(BF)

    peers = [to_cols[2], to_row, to_diag]
    slots = [(2, r), (0, 1 - r), (2, 1 - r)]

    def dp_copy(i):
        dst = dp_all.at[(2, 0, 2, 1)[i], mine]
        return remote(
            dp_all.at[0, mine], dst, gs.at[i], gr.at[i], to_cols[1] if i == 3 else peers[i]
        )

    def dp_relay(i):
        col, rr = slots[i]
        return remote(
            dp_all.at[col, dp_rows(rr)],
            dp_all.at[col + 1, dp_rows(rr)],
            gs.at[4 + i],
            gr.at[4 + i],
            to_cols[1],
        )

    def dp_arrival(i):
        col, rr = (1, r) if i == 3 else slots[i % 4]
        col = col + 1 if i > 3 else col
        ref = dp_all.at[col, dp_rows(rr)]
        remote(ref, ref, gs.at[i], gr.at[i], to_cols[1]).wait_recv()

    for i in (2, 1, 0, 3):
        go(dp_copy(i))

    for t in range(2, yl + 1):
        for round_columns in columns:
            for column in round_columns:
                y_round(*w_column(*column), t)
    sib_w.wait_recv()

    def dx_half(rr):
        rows = dp_rows(rr)
        blk = min(256, depth)

        def turn(j, carry):
            start = pl.multiple_of(j * blk, blk)
            acc = dot_nt(dp_all[0, rows, :], wv[pl.ds(c * depth + start, blk), :])
            for i in range(1, 4):
                acc = acc + dot_nt(dp_all[i, rows, :], w_x[i - 1, pl.ds(start, blk), :])
            dx_ref[rows, pl.ds(start, blk)] = acc.astype(BF)
            return carry

        lax.fori_loop(0, depth // blk, turn, 0)

    dp_arrival(0)
    go(dp_relay(0))
    dp_arrival(1)
    go(dp_relay(1))
    dp_arrival(2)
    go(dp_relay(2))
    dp_arrival(3)
    dp_arrival(4)
    dx_half(r)
    dp_arrival(5)
    dp_arrival(6)
    dx_half(1 - r)

    for d in range(1, ny):

        @pl.when(y + d < ny)
        def _():
            kv_send(d, 0).wait_send()
            kv_send(d, 1).wait_send()

    def sent_turn(yy, carry):
        dkv_send(yy).wait_send()
        return carry

    lax.fori_loop(0, y, sent_turn, 0)
    for copy in seeds + [sib_w, sib_wo] + started:
        copy.wait_send()
    for k in range(CHUNKS):
        token_copy(0, k).wait_send()
        token_copy(1, k).wait_send()


def body(nz, tokens, input_weight, output_weight, output_cotangent):
    ny = lax.axis_size("seq") // nz
    rows, depth = tokens.shape
    n = input_weight.shape[1]
    width = output_cotangent.shape[1]
    hbm = pl.BlockSpec(memory_space=pl.ANY)
    vm = pl.BlockSpec(memory_space=pltpu.VMEM)
    nk, nq = ny * 2 * HEAD, nz * HEAD
    V = pltpu.VMEM
    sem = pltpu.SemaphoreType.DMA
    zl, zsh = ring(nz)
    yl, ysh = ring(ny)
    return pl.pallas_call(
        functools.partial(layer_kernel, ny, nz),
        out_shape=(
            jax.ShapeDtypeStruct(output_cotangent.shape, BF),
            jax.ShapeDtypeStruct(tokens.shape, BF),
        ),
        in_specs=[hbm] * 4,
        out_specs=(vm, vm),
        scratch_shapes=[
            V((4, rows, depth), BF),
            V((4 * depth, n), BF),
            V((HEAD, n), F32),
            V((HEAD, n), F32),
            V((3, depth, n), BF),
            V((4, HEAD, width), BF),
            V((nq, HEAD), BF),
            V((nk, 2 * HEAD), BF),
            V((nq, HEAD), BF),
            V((HEAD, width), BF),
            V((4, HEAD, HEAD), F32),
            V((4, HEAD, HEAD), F32),
            V((nk, nq), F32),
            V((nz, HEAD, HEAD), BF),
            V((nz, HEAD, HEAD), BF),
            V((nz, 8, HEAD), F32),
            V((nz, 8, HEAD), F32),
            V((8, HEAD), F32),
            V((nz, 8, HEAD), F32),
            V((4, HEAD, HEAD), BF),
            V((nz, HEAD, HEAD), BF),
            V((nz, HEAD, HEAD), BF),
            V((2 * HEAD, 2 * HEAD), F32),
            V((nk, 2 * HEAD), BF),
            V((nk, 2 * HEAD), BF),
            V((HEAD, 2 * HEAD), BF),
            V((HEAD, 2 * HEAD), BF),
            V((4, 2 * HEAD, n), BF),
            sem((4,)),
            sem((2, 2)),
            sem((2, 2)),
            sem((2, zl + 1)),
            sem((2, zl + 1)),
            sem((nz, 2, yl + 1)),
            sem((nz, 2, yl + 1)),
            sem((2, yl + 1)),
            sem((2, yl + 1)),
            sem((2, zl + 1)),
            sem((2, zl + 1)),
            sem((2,)),
            sem((2,)),
            sem((3, CHUNKS)),
            sem((3, CHUNKS)),
            sem((CHUNKS // 2,)),
            sem((CHUNKS // 2,)),
            sem((6, nz)),
            sem((6, nz)),
            sem((1 + 2 * ny + 2,)),
            sem((2 * ny + 1,)),
            sem((2, 4)),
            sem((2, 4)),
            sem((ny + 1,)),
            sem((ny + 1,)),
            sem((7,)),
            sem((7,)),
        ],
        compiler_params=pltpu.CompilerParams(
            collective_id=0, has_side_effects=True, vmem_limit_bytes=60 * 2**20
        ),
        cost_estimate=pl.CostEstimate(
            flops=6_000_000_000, bytes_accessed=20_000_000, transcendentals=2_000_000
        ),
        name="layer",
    )(tokens, input_weight, output_weight, output_cotangent)


def solution(mesh):
    seq = mesh.shape["seq"]
    nz = 8 if seq % 32 == 0 else seq // 2
    return jax.shard_map(
        functools.partial(body, nz),
        mesh=mesh,
        in_specs=(
            P("seq", ("row", "col")),
            P("row", "col"),
            P("col", None),
            P(("seq", "row"), "col"),
        ),
        out_specs=(P(("seq", "row"), "col"), P("seq", ("row", "col"))),
        check_vma=False,
    )
```

time: 189 us -> 104 us (0.55); the launches traced: 186 us -> 104 us
  waiting for transfers between devices: 67.6 us -> 0 us
  between operations: 14.1 us -> 0.64 us
  local copies, waits for them, and re-layouts: 6.51 us -> 4.13 us
    all_gather x2 -> x0, waiting for transfers between devices: 66.9 us -> none  [the longest x1 43.5 us: body(): wo_other = lax.all_gather(seed_wo, 'seq', axis=0, tiled=True)]
    unnamed x13 -> x2, local copies, waits for them, and re-layouts: 6.51 us -> 4.13 us
    pallas_call x4 -> x1, Pallas kernels: 97.3 us -> 99 us  [body(): pl.pallas_call(functools.partial(layer_kernel, ny, nz), out_shape=(jax.Sh...]
  transfers between devices with their start and end apart: 2 -> 0, of which waited for: 2 -> 0; matrix products, arithmetic and copies ran while one was open for 0% -> 0% of each run, Pallas kernels for 44% -> 0%
where the time goes in v2:
time: 104 us
  Pallas kernels  99 us (95%)
  local copies, waits for them, and re-layouts  4.13 us (4%)
    pallas_call x1, Pallas kernels, body(): pl.pallas_call(functools.partial(layer_kernel, ny, nz), out_shape=(jax.Sh...  99 us
    unnamed x2, local copies, waits for them, and re-layouts  4.13 us

profile of v2, /device:TPU:1, one launch (start us, length us, event | category | flops | bytes accessed | tf_op | source)
XLA Modules:
  0.0 103.7 jit_solution(15168847085326470402)
XLA Ops:
  0.6 99.0 %layer.1 = (bf16[128,3072]{1,0:T(8,128)(2,1)}, bf16[256,1536]{1,0:T(8,128)(2,1)}) custom-call(bf16[256,1536]{1,0:T(8,128)(2,1)} %t_ref.1, bf16[6144,384]{1,0:T(8,128)(2,1)} %w_ref.1, bf16[128,12288]{1,0:T(8,128)(2,1)} %wo_ref.1, bf16[128,3072]{1,0:T(8,128)(2,1)} %do_ref.1), custom_call_target="tpu_custom_call" | custom-call | flops 6000000000 | bytes 20000000 | tf_op jit(solution)/shard_map/layer/pallas_call | solution.py:713
  99.6 2.1 %copy.8 = bf16[128,3072]{1,0:T(8,128)(2,1)} copy(bf16[128,3072]{1,0:T(8,128)(2,1)} %get-tuple-element.4) | data formatting | bytes 1572864
  101.7 2.1 %copy.9 = bf16[256,1536]{1,0:T(8,128)(2,1)} copy(bf16[256,1536]{1,0:T(8,128)(2,1)} %get-tuple-element.5) | data formatting | bytes 1572864

commit v3 on v2

--- a/solution.py
+++ b/solution.py
@@ -89,8 +89,6 @@
     dkv_own,
     dkv_snd,
     dkv_rcv,
-    row_snd,
-    row_rcv,
     dp_all,
     lsem,
     sds,
@@ -99,8 +97,6 @@
     wzr,
     wys,
     wyr,
-    oys,
-    oyr,
     ozs,
     ozr,
     sbs,
@@ -109,6 +105,10 @@
     tkr,
     pts,
     ptr,
+    qs,
+    qr,
+    uzs,
+    uzr,
     zs,
     zr,
     kvs,
@@ -157,34 +157,29 @@
     greet(
         [dev_z(wrap(z + d, nz)) for d in range(1, nz)]
         + [dev_y(wrap(y + d, ny)) for d in range(1, ny)]
+        + [(wrap(y + d, ny) * nz + z, 1 - r, c) for d in range(1, ny)]
         + [to_row]
         + to_cols[1:]
-        + [to_diag]
+        + [to_diag, (s, 1 - r, cols[3])]
     )
 
     piece = depth // (ny * nz)
     orow = HEAD // nz
-    part = width // ny
+    half_width = width // 2
 
     def w_piece(yy, zz):
         start = pl.multiple_of((yy * nz + zz) * piece, 16)
         return w_x.at[pl.ds(1, 2), pl.ds(start, piece), :]
 
-    def o_piece(yy, zz):
-        return wo_v.at[
-            pl.ds(2, 2),
-            pl.ds(pl.multiple_of(zz * orow, 16), orow),
-            pl.ds(pl.multiple_of(yy * part, 128), part),
-        ]
-
-    def o_super(zz):
-        return wo_v.at[pl.ds(2, 2), pl.ds(pl.multiple_of(zz * orow, 16), orow), :]
-
-    seeds = []
+    def o_piece(zz):
+        rows = pl.ds(pl.multiple_of(zz * orow, 16), orow)
+        return wo_v.at[pl.ds(2, 2), rows, pl.ds(0, half_width)]
+
+    w_seeds, o_seeds, o_direct = [], [], []
     for h in range(2):
         p = cols[2 + h]
         start = pl.multiple_of(s * piece, 16)
-        seeds.append(
+        w_seeds.append(
             remote(
                 w_ref.at[pl.ds(pl.multiple_of(p * depth + s * piece, 16), piece), :],
                 w_x.at[1 + h, pl.ds(start, piece), :],
@@ -194,16 +189,26 @@
             )
         )
         orows = pl.ds(pl.multiple_of(z * orow, 16), orow)
-        seeds.append(
+        o_seeds.append(
             remote(
-                wo_ref.at[orows, pl.ds(pl.multiple_of(p * width + y * part, 128), part)],
-                wo_v.at[2 + h, orows, pl.ds(pl.multiple_of(y * part, 128), part)],
+                wo_ref.at[orows, pl.ds(pl.multiple_of(p * width, 128), half_width)],
+                wo_v.at[2 + h, orows, pl.ds(0, half_width)],
                 sds.at[1, h],
                 sdr.at[1, h],
-                to_cols[2 + h],
+                (s, 1 - r, p),
             )
         )
-    for copy in seeds:
+        o_direct.append(
+            remote(
+                wo_ref.at[:, pl.ds(pl.multiple_of(p * width + half_width, 128), half_width)],
+                wo_v.at[2 + h, :, pl.ds(half_width, half_width)],
+                sds.at[2, h],
+                sdr.at[2, h],
+                (s, 1 - r, p),
+            )
+        )
+    seeds = w_seeds + o_seeds + o_direct
+    for copy in w_seeds + o_seeds:
         copy.start()
 
     def rows_of(k):
@@ -227,6 +232,8 @@
     for k in range(CHUNKS):
         token_copy(0, k).start()
         token_copy(1, k).start()
+    for copy in o_direct:
+        copy.start()
 
     sib_w = remote(
         w_ref.at[pl.ds(pl.multiple_of(cols[1] * depth, 16), depth), :],
@@ -289,9 +296,6 @@
     def w_here(zz):
         return w_piece(y, zz)
 
-    def o_here(yy):
-        return o_piece(yy, z)
-
     def z_start(pick, snd, rcv):
         if zl:
             go(z_ring(pick, snd, rcv, True, 0))
@@ -344,22 +348,26 @@
     def z_rows(zz):
         return pl.ds(pl.multiple_of(zz * HEAD, HEAD), HEAD)
 
-    def kv_rows(yy, rr):
-        return pl.ds(pl.multiple_of(yy * slab + rr * HEAD, HEAD), HEAD)
+    def q_rows(zz, k):
+        return pl.ds(pl.multiple_of(zz * HEAD + k * step, step), step)
+
+    def kv_rows(yy, rr, k):
+        return pl.ds(pl.multiple_of(yy * slab + rr * HEAD + k * step, step), step)
+
+    def token_arrival(kind, k):
+        ref = tbuf.at[(2, 1, 3)[kind], rows_of(k)]
+        remote(ref, ref, tks.at[kind, k], tkr.at[kind, k], to_cols[1]).wait_recv()
+
+    def project_relay(k):
+        token_arrival(0, k)
+        go(token_copy(2, k))
 
     def project(k):
         rows = rows_of(k)
-
-        def arrived(kind):
-            ref = tbuf.at[(2, 1, 3)[kind], rows]
-            remote(ref, ref, tks.at[kind, k], tkr.at[kind, k], to_cols[1]).wait_recv()
-
-        arrived(0)
-        go(token_copy(2, k))
-        arrived(1)
+        token_arrival(1, k)
         acc = product(0, rows, c * depth) + product(1, rows, cols[1] * depth)
         acc = acc + product(2, rows, cols[2] * depth)
-        arrived(2)
+        token_arrival(2, k)
         acc = acc + product(3, rows, cols[3] * depth)
         if k < hk:
             psend[pl.ds(k * step, step), :] = acc
@@ -368,28 +376,74 @@
             part_copy(k - hk).wait_recv()
             out = pl.ds((k - hk) * step, step)
             packed = (acc + precv[out, :]).astype(BF)
-            q_all[pl.ds(pl.multiple_of(z * HEAD + (k - hk) * step, step), step), :] = packed[
-                :, :HEAD
-            ]
-            start = pl.multiple_of(y * slab + r * HEAD + (k - hk) * step, step)
-            kv_all[pl.ds(start, step), :] = packed[:, HEAD:]
-
-    for copy in seeds:
+            q_all[q_rows(z, k - hk), :] = packed[:, :HEAD]
+            kv_all[kv_rows(y, r, k - hk), :] = packed[:, HEAD:]
+
+    def kv_row(k):
+        rows = kv_rows(y, r, k)
+        return remote(kv_all.at[rows], kv_all.at[rows], kvs.at[k, 0], kvr.at[k, 2 * ny], to_row)
+
+    def kv_row_arrival(k):
+        rows = kv_rows(y, 1 - r, k)
+        return remote(kv_all.at[rows], kv_all.at[rows], kvs.at[k, 0], kvr.at[k, 2 * ny], to_row)
+
+    def kv_send(d, other, k):
+        rr = 1 - r if other else r
+        rows = kv_rows(y, rr, k)
+        return remote(
+            kv_all.at[rows],
+            kv_all.at[rows],
+            kvs.at[k, 1 + 2 * d + other],
+            kvr.at[k, 2 * y + other],
+            dev_y(wrap(y + d, ny)),
+        )
+
+    def kv_arrival(yy, other, k):
+        rr = 1 - r if other else r
+        rows = kv_rows(yy, rr, k)
+        return remote(
+            kv_all.at[rows], kv_all.at[rows], kvs.at[k, 0], kvr.at[k, 2 * yy + other], to_row
+        )
+
+    def kv_sends(other, k):
+        for d in range(1, ny):
+
+            @pl.when(y + d < ny)
+            def _():
+                kv_send(d, other, k).start()
+
+    def q_send(d, k):
+        rows = q_rows(z, k)
+        to = wrap(z + d, nz)
+        return remote(q_all.at[rows], q_all.at[rows], qs.at[k, d], qr.at[k, d], dev_z(to))
+
+    def q_arrival(d, k):
+        rows = q_rows(wrap(z - d, nz), k)
+        return remote(q_all.at[rows], q_all.at[rows], qs.at[k, d], qr.at[k, d], dev_z(z_next))
+
+    order = sorted(range(1, nz), key=lambda d: -min(d, nz - d))
+
+    def share(k):
+        go(kv_row(k))
+        kv_sends(0, k)
+        for d in order:
+            go(q_send(d, k))
+
+    for copy in w_seeds:
         copy.wait_recv()
     z_start(w_here, wzs, wzr)
-    y_start(o_here, oys, oyr)
     pick, snd, rcv = w_column(True, 0)
     y_start(pick, snd, rcv)
+    for copy in o_seeds:
+        copy.wait_recv()
+    z_start(o_piece, ozs, ozr)
     columns = [[(True, 0)]]
     own_tokens.wait()
     own_w.wait()
-    for t in range(1, yl + 1):
-        y_round(o_here, oys, oyr, t)
-    z_start(o_super, ozs, ozr)
     for k in range(max(CHUNKS, zl)):
         t = k + 1
         if k < CHUNKS:
-            project(k)
+            project_relay(k)
         if t <= zl:
             ways = z_round(w_here, wzs, wzr, t)
             for long in ways:
@@ -397,195 +451,207 @@
             columns.append([(long, t) for long in ways])
             for column in columns[t - 1]:
                 y_round(*w_column(*column), 1)
-            z_round(o_super, ozs, ozr, t)
-
-    def kv_row():
-        rows = kv_rows(y, r)
-        return remote(kv_all.at[rows], kv_all.at[rows], kvs.at[0], kvr.at[2 * ny], to_row)
-
-    def kv_row_arrival():
-        rows = kv_rows(y, 1 - r)
-        return remote(kv_all.at[rows], kv_all.at[rows], kvs.at[0], kvr.at[2 * ny], to_row)
-
-    def kv_send(d, other):
-        rr = 1 - r if other else r
-        rows = kv_rows(y, rr)
-        return remote(
-            kv_all.at[rows],
-            kv_all.at[rows],
-            kvs.at[1 + 2 * d + other],
-            kvr.at[2 * y + other],
-            dev_y(wrap(y + d, ny)),
-        )
-
-    def kv_arrival(yy, other):
-        rr = 1 - r if other else r
-        rows = kv_rows(yy, rr)
-        return remote(kv_all.at[rows], kv_all.at[rows], kvs.at[0], kvr.at[2 * yy + other], to_row)
-
-    go(kv_row())
-    for d in range(1, ny):
-
-        @pl.when(y + d < ny)
-        def _():
-            kv_send(d, 0).start()
-
-    def z_gather(kind, buf, d):
-        return remote(
-            buf.at[z_rows(z)],
-            buf.at[z_rows(z)],
-            zs.at[kind, d],
-            zr.at[kind, d],
-            dev_z(wrap(z + d, nz)),
-        )
-
-    def z_gather_arrival(kind, buf, d):
-        rows = z_rows(wrap(z - d, nz))
-        return remote(buf.at[rows], buf.at[rows], zs.at[kind, d], zr.at[kind, d], dev_z(z_next))
-
-    def z_give(kind, src, dst, d):
-        to = wrap(z + d, nz)
-        return remote(src.at[to], dst.at[z], zs.at[kind, d], zr.at[kind, d], dev_z(to))
-
-    def z_give_arrival(kind, dst, d):
-        slot = wrap(z - d, nz)
-        return remote(dst.at[slot], dst.at[slot], zs.at[kind, d], zr.at[kind, d], dev_z(z_next))
-
-    order = sorted(range(1, nz), key=lambda d: -min(d, nz - d))
-    for d in order:
-        go(z_gather(0, q_all, d))
+            z_round(o_piece, ozs, ozr, t)
+        if k < CHUNKS:
+            project(k)
+        if hk <= k < CHUNKS:
+            share(k - hk)
 
     for column in columns[zl]:
         y_round(*w_column(*column), 1)
 
-    kv_row_arrival().wait_recv()
-    for d in range(1, ny):
-
-        @pl.when(y + d < ny)
-        def _():
-            kv_send(d, 1).start()
+    for k in range(hk):
+        kv_row_arrival(k).wait_recv()
+        kv_sends(1, k)
 
     own_do.wait()
     own_wo.wait()
     sib_wo.wait_recv()
+    for copy in o_direct:
+        copy.wait_recv()
     for i in range(1, 4):
         ups[i] = dot_nt(do_v[...], wo_v[i])
         go(remote(ups.at[i], upr.at[i], cs.at[0, i], cr.at[0, i], to_cols[i]))
     upr[0] = dot_nt(do_v[...], wo_v[0])
 
     for d in order:
-        z_gather_arrival(0, q_all, d).wait_recv()
-    nq = nz * HEAD
-    lane = lax.broadcasted_iota(jnp.int32, (1, nq), 1)
-    qpos = (y * nz + lane // HEAD) * slab + r * HEAD + lane % HEAD
+        for k in range(hk):
+            q_arrival(d, k).wait_recv()
+    hz = nz // 2
+    hq = hz * HEAD
+    near = z // hz
+    far = 1 - near
+    lane = lax.broadcasted_iota(jnp.int32, (1, hq), 1)
     kofs = lax.broadcasted_iota(jnp.int32, (slab, 1), 0)
 
     def y_rows(yy):
         return pl.ds(pl.multiple_of(yy * slab, slab), slab)
 
-    def score_turn(yy, largest):
-        @pl.when(yy < y)
-        def _():
-            kv_arrival(yy, 0).wait_recv()
-            kv_arrival(yy, 1).wait_recv()
-
-        keys = kv_all[y_rows(yy), :HEAD]
-        scores = dot_nt(keys, q_all[...]) * factor
-        kpos = (yy * nz + z) * slab + kofs
-        scores = jnp.where(kpos <= qpos, scores, masked_score)
-        s_all[y_rows(yy), :] = scores
-        return jnp.maximum(largest, jnp.max(scores, axis=0, keepdims=True))
-
-    largest = lax.fori_loop(0, y + 1, score_turn, jnp.full((1, nq), masked_score, F32))
-
-    def weight_turn(yy, carry):
-        total, mixed = carry
-        weights = jnp.exp(s_all[y_rows(yy), :] - largest)
-        total = total + jnp.sum(weights, axis=0, keepdims=True)
-        mixed = mixed + dot_tn(kv_all[y_rows(yy), HEAD:], weights.astype(BF))
-        return total, mixed
-
-    total, mixed = lax.fori_loop(
-        0, y + 1, weight_turn, (jnp.zeros((1, nq), F32), jnp.zeros((HEAD, nq), F32))
-    )
-    for zz in range(nz):
-        lanes = slice(zz * HEAD, (zz + 1) * HEAD)
-        o_snd[zz] = mixed[:, lanes].astype(BF)
-        st_snd[zz, 0:1, :] = largest[:, lanes]
-        st_snd[zz, 1:2, :] = total[:, lanes]
-    for d in order:
-        go(z_give(1, o_snd, o_rcv, d))
-        go(z_give(2, st_snd, st_rcv, d))
-    o_rcv[z] = o_snd[z]
-    st_rcv[z] = st_snd[z]
-
+    def q_half(half):
+        return pl.ds(pl.multiple_of(half * hq, hq), hq)
+
+    def z_give(kind, src, dst, to):
+        return remote(src.at[to], dst.at[z], zs.at[kind, to], zr.at[kind, z], dev_z(to))
+
+    def z_give_arrival(kind, dst, d):
+        slot = wrap(z - d, nz)
+        remote(
+            dst.at[slot], dst.at[slot], zs.at[kind, slot], zr.at[kind, slot], dev_z(z_next)
+        ).wait_recv()
+
+    def u_piece(zz):
+        return u_all.at[z_rows(zz)]
+
+    def forward(half, first):
+        lanes_of = q_half(half)
+        queries = q_all[lanes_of, :]
+        qpos = (y * nz + half * hz + lane // HEAD) * slab + r * HEAD + lane % HEAD
+
+        def score_turn(yy, largest):
+            if first:
+
+                @pl.when(yy < y)
+                def _():
+                    for k in range(hk):
+                        kv_arrival(yy, 0, k).wait_recv()
+                        kv_arrival(yy, 1, k).wait_recv()
+
+            keys = kv_all[y_rows(yy), :HEAD]
+            scores = dot_nt(keys, queries) * factor
+            kpos = (yy * nz + z) * slab + kofs
+            scores = jnp.where(kpos <= qpos, scores, masked_score)
+            s_all[y_rows(yy), lanes_of] = scores
+            return jnp.maximum(largest, jnp.max(scores, axis=0, keepdims=True))
+
+        largest = lax.fori_loop(0, y + 1, score_turn, jnp.full((1, hq), masked_score, F32))
+
+        def weight_turn(yy, carry):
+            total, mixed = carry
+            weights = jnp.exp(s_all[y_rows(yy), lanes_of] - largest)
+            total = total + jnp.sum(weights, axis=0, keepdims=True)
+            mixed = mixed + dot_tn(kv_all[y_rows(yy), HEAD:], weights.astype(BF))
+            return total, mixed
+
+        total, mixed = lax.fori_loop(
+            0, y + 1, weight_turn, (jnp.zeros((1, hq), F32), jnp.zeros((HEAD, hq), F32))
+        )
+        for j in range(hz):
+            zz = half * hz + j
+            lanes = slice(j * HEAD, (j + 1) * HEAD)
+            o_snd[zz] = mixed[:, lanes].astype(BF)
+            st_snd[zz, 0:1, :] = largest[:, lanes]
+            st_snd[zz, 1:2, :] = total[:, lanes]
+
+            @pl.when(zz != z)
+            def _():
+                z_give(1, o_snd, o_rcv, zz).start()
+                z_give(2, st_snd, st_rcv, zz).start()
+
+    forward(far, True)
     for i in range(1, 4):
         remote(upr.at[i], upr.at[i], cs.at[0, i], cr.at[0, i], to_cols[i]).wait_recv()
     up = (upr[0] + upr[1] + upr[2] + upr[3]).astype(BF)
     u_all[z_rows(z), :] = up
+    z_start(u_piece, uzs, uzr)
+    up_t = up.astype(F32).T
+    forward(near, False)
+    z_round(u_piece, uzs, uzr, 1)
+    o_rcv[z] = o_snd[z]
+    st_rcv[z] = st_snd[z]
+    z_round(u_piece, uzs, uzr, 2)
+
     for d in order:
-        go(z_gather(3, u_all, d))
-    up_t = up.astype(F32).T
-
-    for d in order:
-        z_give_arrival(2, st_rcv, d).wait_recv()
-        z_give_arrival(1, o_rcv, d).wait_recv()
+        z_give_arrival(2, st_rcv, d)
     top = st_rcv[0, 0:1, :]
     for zz in range(1, nz):
         top = jnp.maximum(top, st_rcv[zz, 0:1, :])
     full_total = jnp.zeros((1, HEAD), F32)
-    full = jnp.zeros((HEAD, HEAD), F32)
     for zz in range(nz):
-        scale = jnp.exp(st_rcv[zz, 0:1, :] - top)
-        full_total = full_total + scale * st_rcv[zz, 1:2, :]
-        full = full + scale * o_rcv[zz].astype(F32)
+        full_total = full_total + jnp.exp(st_rcv[zz, 0:1, :] - top) * st_rcv[zz, 1:2, :]
+    full = jnp.exp(st_rcv[z, 0:1, :] - top) * o_rcv[z].astype(F32)
+    for d in order:
+        z_give_arrival(1, o_rcv, d)
+        slot = wrap(z - d, nz)
+        full = full + jnp.exp(st_rcv[slot, 0:1, :] - top) * o_rcv[slot].astype(F32)
     att_t = (full / full_total).astype(BF).astype(F32)
     ld_snd[0:1, :] = top + jnp.log(full_total)
     ld_snd[1:2, :] = jnp.sum(up_t * att_t, axis=0, keepdims=True)
     ld_rcv[z] = ld_snd[...]
     for d in order:
-        go(remote(ld_snd, ld_rcv.at[z], zs.at[4, d], zr.at[4, d], dev_z(wrap(z + d, nz))))
+        to = wrap(z + d, nz)
+        go(remote(ld_snd, ld_rcv.at[z], zs.at[3, to], zr.at[3, z], dev_z(to)))
+    for t in range(3, zl + 1):
+        z_round(u_piece, uzs, uzr, t)
     att_all[0] = att_t.T.astype(BF)
     for i in range(1, 4):
         go(remote(att_all.at[0], att_all.at[i], cs.at[1, i], cr.at[1, i], to_cols[i]))
 
     for d in order:
-        z_gather_arrival(3, u_all, d).wait_recv()
-        z_give_arrival(4, ld_rcv, d).wait_recv()
-    logsum = jnp.concatenate([ld_rcv[zz, 0:1, :] for zz in range(nz)], axis=1)
-    delta = jnp.concatenate([ld_rcv[zz, 1:2, :] for zz in range(nz)], axis=1)
-
-    def dkv_send(yy):
+        z_give_arrival(3, ld_rcv, d)
+
+    def half_rows(yy, rr):
+        return pl.ds(pl.multiple_of(yy * slab + rr * HEAD, HEAD), HEAD)
+
+    def dkv_send(yy, rr):
         return remote(
-            dkv_snd.at[y_rows(yy)], dkv_rcv.at[y_rows(y)], ds.at[yy], dr.at[y], dev_y(yy)
-        )
-
-    def grad_turn(yy, dq):
-        keys, values = kv_all[y_rows(yy), :HEAD], kv_all[y_rows(yy), HEAD:]
-        probs = jnp.exp(s_all[y_rows(yy), :] - logsum)
-        prob_grad = dot_nt(values, u_all[...])
-        score_grad = (probs * (prob_grad - delta)).astype(BF)
-        dk = jnp.dot(score_grad, q_all[...], preferred_element_type=F32) * factor
-        dv = jnp.dot(probs.astype(BF), u_all[...], preferred_element_type=F32)
-        dkv_own[:, :HEAD] = dk
-        dkv_own[:, HEAD:] = dv
-
-        @pl.when(yy < y)
-        def _():
-            dkv_snd[y_rows(yy), :] = dkv_own[...].astype(BF)
-            dkv_send(yy).start()
-
-        return dq + dot_tn(keys, score_grad)
-
-    dq = lax.fori_loop(0, y + 1, grad_turn, jnp.zeros((HEAD, nq), F32))
-    for zz in range(nz):
-        dq_snd[zz] = (dq[:, zz * HEAD : (zz + 1) * HEAD] * factor).astype(BF)
-    for d in order:
-        go(z_give(5, dq_snd, dq_rcv, d))
+            dkv_snd.at[half_rows(yy, rr)],
+            dkv_rcv.at[half_rows(y, r)],
+            ds.at[yy, rr],
+            dr.at[2 * y + r],
+            (yy * nz + z, rr, c),
+        )
+
+    def backward(half, first):
+        lanes_of = q_half(half)
+        queries, upstream = q_all[lanes_of, :], u_all[lanes_of, :]
+        logsum = jnp.concatenate([ld_rcv[half * hz + j, 0:1, :] for j in range(hz)], axis=1)
+        delta = jnp.concatenate([ld_rcv[half * hz + j, 1:2, :] for j in range(hz)], axis=1)
+
+        def grad_turn(yy, dq):
+            keys, values = kv_all[y_rows(yy), :HEAD], kv_all[y_rows(yy), HEAD:]
+            probs = jnp.exp(s_all[y_rows(yy), lanes_of] - logsum)
+            prob_grad = dot_nt(values, upstream)
+            score_grad = (probs * (prob_grad - delta)).astype(BF)
+            dk = jnp.dot(score_grad, queries, preferred_element_type=F32) * factor
+            dv = jnp.dot(probs.astype(BF), upstream, preferred_element_type=F32)
+            if first:
+                dkv_own[y_rows(yy), :HEAD] = dk
+                dkv_own[y_rows(yy), HEAD:] = dv
+            else:
+                dk = dk + dkv_own[y_rows(yy), :HEAD]
+                dv = dv + dkv_own[y_rows(yy), HEAD:]
+                dkv_snd[y_rows(yy), :HEAD] = dk.astype(BF)
+                dkv_snd[y_rows(yy), HEAD:] = dv.astype(BF)
+
+                @pl.when(yy < y)
+                def _():
+                    dkv_send(yy, r).start()
+
+                dkv_send(yy, 1 - r).start()
+
+                @pl.when(yy == y)
+                def _():
+                    dkv_own[y_rows(yy), :HEAD] = dk
+                    dkv_own[y_rows(yy), HEAD:] = dv
+
+            return dq + dot_tn(keys, score_grad)
+
+        dq = lax.fori_loop(0, y + 1, grad_turn, jnp.zeros((HEAD, hq), F32))
+        for j in range(hz):
+            zz = half * hz + j
+            dq_snd[zz] = (dq[:, j * HEAD : (j + 1) * HEAD] * factor).astype(BF)
+
+            @pl.when(zz != z)
+            def _():
+                z_give(4, dq_snd, dq_rcv, zz).start()
+
+    backward(far, True)
+    backward(near, False)
 
     for i in range(1, 4):
         remote(att_all.at[i], att_all.at[i], cs.at[1, i], cr.at[1, i], to_cols[i]).wait_recv()
-    for j in range(ny):
+    for j in range(4):
+        part = width // 4
         lanes = pl.ds(j * part, part)
         total_out = jnp.dot(att_all[0], wo_v[0, :, lanes], preferred_element_type=F32)
         for i in range(1, 4):
@@ -594,29 +660,30 @@
             )
         out_ref[:, lanes] = total_out.astype(BF)
 
+    def dp_rows(rr):
+        return pl.ds(pl.multiple_of(rr * HEAD, HEAD), HEAD)
+
+    mine = dp_rows(r)
+    dq_sum = dq_snd[z].astype(F32)
+    for d in order:
+        z_give_arrival(4, dq_rcv, d)
+        dq_sum = dq_sum + dq_rcv[wrap(z - d, nz)].astype(F32)
+    dp_all[0, mine, :HEAD] = dq_sum.T.astype(BF)
+
+    def dkv_arrival(yy, rr):
+        ref = dkv_rcv.at[half_rows(yy, rr)]
+        remote(ref, ref, ds.at[0, 0], dr.at[2 * yy + rr], to_row).wait_recv()
+        dkv_own[half_rows(y, r), :] += dkv_rcv[half_rows(yy, rr), :].astype(F32)
+
+    dkv_arrival(y, 1 - r)
     for d in range(1, ny):
 
         @pl.when(y + d < ny)
         def _():
-            yy = wrap(y + d, ny)
-            ref = dkv_rcv.at[y_rows(yy)]
-            remote(ref, ref, ds.at[0], dr.at[yy], to_row).wait_recv()
-            dkv_own[...] += dkv_rcv[y_rows(yy), :].astype(F32)
-
-    def dp_rows(rr):
-        return pl.ds(pl.multiple_of(rr * HEAD, HEAD), HEAD)
-
-    mine, theirs = dp_rows(r), dp_rows(1 - r)
-    row_snd[...] = dkv_own[theirs, :].astype(BF)
-    row_copy = remote(row_snd, row_rcv, ds.at[ny], dr.at[ny], to_row)
-    go(row_copy)
-    dq_sum = dq_snd[z].astype(F32)
-    for d in order:
-        z_give_arrival(5, dq_rcv, d).wait_recv()
-        dq_sum = dq_sum + dq_rcv[wrap(z - d, nz)].astype(F32)
-    dp_all[0, mine, :HEAD] = dq_sum.T.astype(BF)
-    row_copy.wait_recv()
-    dp_all[0, mine, HEAD:] = (dkv_own[mine, :] + row_rcv[...].astype(F32)).astype(BF)
+            dkv_arrival(wrap(y + d, ny), r)
+            dkv_arrival(wrap(y + d, ny), 1 - r)
+
+    dp_all[0, mine, HEAD:] = dkv_own[half_rows(y, r), :].astype(BF)
 
     peers = [to_cols[2], to_row, to_diag]
     slots = [(2, r), (0, 1 - r), (2, 1 - r)]
@@ -683,14 +750,25 @@
 
         @pl.when(y + d < ny)
         def _():
-            kv_send(d, 0).wait_send()
-            kv_send(d, 1).wait_send()
+            for k in range(hk):
+                kv_send(d, 0, k).wait_send()
+                kv_send(d, 1, k).wait_send()
 
     def sent_turn(yy, carry):
-        dkv_send(yy).wait_send()
+        dkv_send(yy, 1 - r).wait_send()
+
+        @pl.when(yy < y)
+        def _():
+            dkv_send(yy, r).wait_send()
+
         return carry
 
-    lax.fori_loop(0, y, sent_turn, 0)
+    lax.fori_loop(0, y + 1, sent_turn, 0)
+    for d in order:
+        to = wrap(z + d, nz)
+        z_give(1, o_snd, o_rcv, to).wait_send()
+        z_give(2, st_snd, st_rcv, to).wait_send()
+        z_give(4, dq_snd, dq_rcv, to).wait_send()
     for copy in seeds + [sib_w, sib_wo] + started:
         copy.wait_send()
     for k in range(CHUNKS):
@@ -741,21 +819,17 @@
             V((4, HEAD, HEAD), BF),
             V((nz, HEAD, HEAD), BF),
             V((nz, HEAD, HEAD), BF),
-            V((2 * HEAD, 2 * HEAD), F32),
+            V((nk, 2 * HEAD), F32),
             V((nk, 2 * HEAD), BF),
             V((nk, 2 * HEAD), BF),
-            V((HEAD, 2 * HEAD), BF),
-            V((HEAD, 2 * HEAD), BF),
             V((4, 2 * HEAD, n), BF),
             sem((4,)),
-            sem((2, 2)),
-            sem((2, 2)),
+            sem((3, 2)),
+            sem((3, 2)),
             sem((2, zl + 1)),
             sem((2, zl + 1)),
             sem((nz, 2, yl + 1)),
             sem((nz, 2, yl + 1)),
-            sem((2, yl + 1)),
-            sem((2, yl + 1)),
             sem((2, zl + 1)),
             sem((2, zl + 1)),
             sem((2,)),
@@ -764,19 +838,23 @@
             sem((3, CHUNKS)),
             sem((CHUNKS // 2,)),
             sem((CHUNKS // 2,)),
-            sem((6, nz)),
-            sem((6, nz)),
-            sem((1 + 2 * ny + 2,)),
-            sem((2 * ny + 1,)),
+            sem((CHUNKS // 2, nz)),
+            sem((CHUNKS // 2, nz)),
+            sem((2, zl + 1)),
+            sem((2, zl + 1)),
+            sem((5, nz)),
+            sem((5, nz)),
+            sem((CHUNKS // 2, 2 * ny + 1)),
+            sem((CHUNKS // 2, 2 * ny + 1)),
             sem((2, 4)),
             sem((2, 4)),
-            sem((ny + 1,)),
-            sem((ny + 1,)),
+            sem((ny, 2)),
+            sem((2 * ny,)),
             sem((7,)),
             sem((7,)),
         ],
         compiler_params=pltpu.CompilerParams(
-            collective_id=0, has_side_effects=True, vmem_limit_bytes=60 * 2**20
+            collective_id=0, has_side_effects=True, vmem_limit_bytes=52 * 2**20
         ),
         cost_estimate=pl.CostEstimate(
             flops=6_000_000_000, bytes_accessed=20_000_000, transcendentals=2_000_000

time: 104 us -> 90.7 us (0.87)
  Pallas kernels: 99 us -> 88.2 us
  local copies, waits for them, and re-layouts: 4.13 us -> 1.76 us
    pallas_call x1, Pallas kernels: 99 us -> 88.2 us  [body(): pl.pallas_call(functools.partial(layer_kernel, ny, nz), out_shape=(jax.Sh...]
    unnamed x2, local copies, waits for them, and re-layouts: 4.13 us -> 1.76 us
where the time goes in v3:
time: 90.7 us; the launch traced here: 90.6 us
  Pallas kernels  88.2 us (97%)
  local copies, waits for them, and re-layouts  1.76 us (2%)
    pallas_call x1, Pallas kernels, body(): pl.pallas_call(functools.partial(layer_kernel, ny, nz), out_shape=(jax.Sh...  88.2 us

profile of v3, /device:TPU:1, one launch (start us, length us, event | category | flops | bytes accessed | tf_op | source)
XLA Modules:
  0.0 90.6 jit_solution(4815151588568020516)
XLA Ops:
  0.6 88.2 %layer.1 = (bf16[128,3072]{1,0:T(8,128)(2,1)S(1)}, bf16[256,1536]{1,0:T(8,128)(2,1)S(1)}) custom-call(bf16[256,1536]{1,0:T(8,128)(2,1)} %t_ref.1, bf16[6144,384]{1,0:T(8,128)(2,1)} %w_ref.1, bf16[128,12288]{1,0:T(8,128)(2,1)} %wo_ref.1, bf16[128,3072]{1,0:T(8,128)(2,1)} %do_ref.1), custom_call_target="tpu_custom_call" | custom-call | flops 6000000000 | bytes 20000000 | tf_op jit(solution)/shard_map/layer/pallas_call | solution.py:791
  88.9 0.9 copy.8
  89.7 0.9 copy.9

commit v4 on v3

--- a/solution.py
+++ b/solution.py
@@ -14,6 +14,7 @@
 BF = jnp.bfloat16
 F32 = jnp.float32
 CHUNKS = 4
+AHEAD = 2
 
 
 def remote(src, dst, send_sem, recv_sem, device):
@@ -81,8 +82,10 @@
     o_rcv,
     st_snd,
     st_rcv,
-    ld_snd,
-    ld_rcv,
+    st_rows,
+    o_all,
+    o_scale,
+    ld,
     att_all,
     dq_snd,
     dq_rcv,
@@ -90,6 +93,7 @@
     dkv_snd,
     dkv_rcv,
     dp_all,
+    dx_acc,
     lsem,
     sds,
     sdr,
@@ -107,8 +111,6 @@
     ptr,
     qs,
     qr,
-    uzs,
-    uzr,
     zs,
     zr,
     kvs,
@@ -229,8 +231,9 @@
             tbuf.at[2, rows], tbuf.at[3, rows], tks.at[2, k], tkr.at[2, k], to_cols[1]
         )
 
+    for k in range(AHEAD):
+        token_copy(0, k).start()
     for k in range(CHUNKS):
-        token_copy(0, k).start()
         token_copy(1, k).start()
     for copy in o_direct:
         copy.start()
@@ -442,8 +445,6 @@
     own_w.wait()
     for k in range(max(CHUNKS, zl)):
         t = k + 1
-        if k < CHUNKS:
-            project_relay(k)
         if t <= zl:
             ways = z_round(w_here, wzs, wzr, t)
             for long in ways:
@@ -453,6 +454,9 @@
                 y_round(*w_column(*column), 1)
             z_round(o_piece, ozs, ozr, t)
         if k < CHUNKS:
+            project_relay(k)
+            if k + AHEAD < CHUNKS:
+                token_copy(0, k + AHEAD).start()
             project(k)
         if hk <= k < CHUNKS:
             share(k - hk)
@@ -499,10 +503,7 @@
             dst.at[slot], dst.at[slot], zs.at[kind, slot], zr.at[kind, slot], dev_z(z_next)
         ).wait_recv()
 
-    def u_piece(zz):
-        return u_all.at[z_rows(zz)]
-
-    def forward(half, first):
+    def score(half, first):
         lanes_of = q_half(half)
         queries = q_all[lanes_of, :]
         qpos = (y * nz + half * hz + lane // HEAD) * slab + r * HEAD + lane % HEAD
@@ -523,7 +524,10 @@
             s_all[y_rows(yy), lanes_of] = scores
             return jnp.maximum(largest, jnp.max(scores, axis=0, keepdims=True))
 
-        largest = lax.fori_loop(0, y + 1, score_turn, jnp.full((1, hq), masked_score, F32))
+        return lax.fori_loop(0, y + 1, score_turn, jnp.full((1, hq), masked_score, F32))
+
+    def weigh(half, largest):
+        lanes_of = q_half(half)
 
         def weight_turn(yy, carry):
             total, mixed = carry
@@ -535,59 +539,67 @@
         total, mixed = lax.fori_loop(
             0, y + 1, weight_turn, (jnp.zeros((1, hq), F32), jnp.zeros((HEAD, hq), F32))
         )
-        for j in range(hz):
-            zz = half * hz + j
-            lanes = slice(j * HEAD, (j + 1) * HEAD)
-            o_snd[zz] = mixed[:, lanes].astype(BF)
-            st_snd[zz, 0:1, :] = largest[:, lanes]
-            st_snd[zz, 1:2, :] = total[:, lanes]
-
-            @pl.when(zz != z)
-            def _():
-                z_give(1, o_snd, o_rcv, zz).start()
-                z_give(2, st_snd, st_rcv, zz).start()
-
-    forward(far, True)
+        st_rows[0:1, lanes_of] = largest
+        st_rows[1:2, lanes_of] = total
+        o_all[:, lanes_of] = mixed
+
+    top_far = score(far, True)
+
     for i in range(1, 4):
         remote(upr.at[i], upr.at[i], cs.at[0, i], cr.at[0, i], to_cols[i]).wait_recv()
-    up = (upr[0] + upr[1] + upr[2] + upr[3]).astype(BF)
-    u_all[z_rows(z), :] = up
-    z_start(u_piece, uzs, uzr)
-    up_t = up.astype(F32).T
-    forward(near, False)
-    z_round(u_piece, uzs, uzr, 1)
+    u_all[z_rows(z), :] = (upr[0] + upr[1] + upr[2] + upr[3]).astype(BF)
+    for d in order:
+        to = wrap(z + d, nz)
+        rows = z_rows(z)
+        go(remote(u_all.at[rows], u_all.at[rows], zs.at[0, to], zr.at[0, z], dev_z(to)))
+    top_near = score(near, False)
+    weigh(far, top_far)
+    weigh(near, top_near)
+
+    for zz in range(nz):
+        lanes = slice(zz * HEAD, (zz + 1) * HEAD)
+        o_snd[zz] = o_all[:, lanes].astype(BF)
+        st_snd[0, zz : zz + 1, :] = st_rows[0:1, lanes]
+        st_snd[1, zz : zz + 1, :] = st_rows[1:2, lanes]
+    for d in order:
+        slot = wrap(z - d, nz)
+        ref = u_all.at[z_rows(slot)]
+        remote(ref, ref, zs.at[0, slot], zr.at[0, slot], dev_z(z_next)).wait_recv()
+    for zz in range(nz):
+        lanes = slice(zz * HEAD, (zz + 1) * HEAD)
+        up_t = u_all[lanes, :].astype(F32).T
+        st_snd[2, zz : zz + 1, :] = jnp.sum(up_t * o_all[:, lanes], axis=0, keepdims=True)
+
+    def st_copy(to):
+        return remote(st_snd, st_rcv.at[z], zs.at[2, to], zr.at[2, z], dev_z(to))
+
+    for d in order:
+        st_copy(wrap(z + d, nz)).start()
+    for d in order:
+        z_give(1, o_snd, o_rcv, wrap(z + d, nz)).start()
     o_rcv[z] = o_snd[z]
-    st_rcv[z] = st_snd[z]
-    z_round(u_piece, uzs, uzr, 2)
-
+    st_rcv[z] = st_snd[...]
     for d in order:
         z_give_arrival(2, st_rcv, d)
-    top = st_rcv[0, 0:1, :]
+    top = st_rcv[0, 0]
     for zz in range(1, nz):
-        top = jnp.maximum(top, st_rcv[zz, 0:1, :])
-    full_total = jnp.zeros((1, HEAD), F32)
+        top = jnp.maximum(top, st_rcv[zz, 0])
+    full_total = jnp.zeros((nz, HEAD), F32)
+    full_delta = jnp.zeros((nz, HEAD), F32)
     for zz in range(nz):
-        full_total = full_total + jnp.exp(st_rcv[zz, 0:1, :] - top) * st_rcv[zz, 1:2, :]
-    full = jnp.exp(st_rcv[z, 0:1, :] - top) * o_rcv[z].astype(F32)
-    for d in order:
-        z_give_arrival(1, o_rcv, d)
-        slot = wrap(z - d, nz)
-        full = full + jnp.exp(st_rcv[slot, 0:1, :] - top) * o_rcv[slot].astype(F32)
-    att_t = (full / full_total).astype(BF).astype(F32)
-    ld_snd[0:1, :] = top + jnp.log(full_total)
-    ld_snd[1:2, :] = jnp.sum(up_t * att_t, axis=0, keepdims=True)
-    ld_rcv[z] = ld_snd[...]
-    for d in order:
-        to = wrap(z + d, nz)
-        go(remote(ld_snd, ld_rcv.at[z], zs.at[3, to], zr.at[3, z], dev_z(to)))
-    for t in range(3, zl + 1):
-        z_round(u_piece, uzs, uzr, t)
-    att_all[0] = att_t.T.astype(BF)
-    for i in range(1, 4):
-        go(remote(att_all.at[0], att_all.at[i], cs.at[1, i], cr.at[1, i], to_cols[i]))
-
-    for d in order:
-        z_give_arrival(3, ld_rcv, d)
+        scale = jnp.exp(st_rcv[zz, 0] - top)
+        full_total = full_total + scale * st_rcv[zz, 1]
+        full_delta = full_delta + scale * st_rcv[zz, 2]
+        o_scale[zz] = scale
+    all_logsum = top + jnp.log(full_total)
+    all_delta = full_delta / full_total
+    for zz in range(nz):
+        row = slice(zz, zz + 1)
+        ld[zz, 0:1, :] = all_logsum[row]
+        ld[zz, 1:2, :] = all_delta[row]
+        ld[zz, 2:3, :] = full_total[row]
+        for other in range(nz):
+            ld[zz, 8 + other : 9 + other, :] = o_scale[other, row, :]
 
     def half_rows(yy, rr):
         return pl.ds(pl.multiple_of(yy * slab + rr * HEAD, HEAD), HEAD)
@@ -604,8 +616,8 @@
     def backward(half, first):
         lanes_of = q_half(half)
         queries, upstream = q_all[lanes_of, :], u_all[lanes_of, :]
-        logsum = jnp.concatenate([ld_rcv[half * hz + j, 0:1, :] for j in range(hz)], axis=1)
-        delta = jnp.concatenate([ld_rcv[half * hz + j, 1:2, :] for j in range(hz)], axis=1)
+        logsum = jnp.concatenate([ld[half * hz + j, 0:1, :] for j in range(hz)], axis=1)
+        delta = jnp.concatenate([ld[half * hz + j, 1:2, :] for j in range(hz)], axis=1)
 
         def grad_turn(yy, dq):
             keys, values = kv_all[y_rows(yy), :HEAD], kv_all[y_rows(yy), HEAD:]
@@ -648,6 +660,108 @@
     backward(far, True)
     backward(near, False)
 
+    full = jnp.zeros((HEAD, HEAD), F32)
+    for d in order:
+        z_give_arrival(1, o_rcv, d)
+    for zz in range(nz):
+        full = full + ld[z, 8 + zz : 9 + zz, :] * o_rcv[zz].astype(F32)
+    att_all[0] = (full / ld[z, 2:3, :]).T.astype(BF)
+    for i in range(1, 4):
+        go(remote(att_all.at[0], att_all.at[i], cs.at[1, i], cr.at[1, i], to_cols[i]))
+
+    def dp_rows(rr):
+        return pl.ds(pl.multiple_of(rr * HEAD, HEAD), HEAD)
+
+    mine, theirs = dp_rows(r), dp_rows(1 - r)
+
+    def dkv_arrival(yy, rr):
+        ref = dkv_rcv.at[half_rows(yy, rr)]
+        remote(ref, ref, ds.at[0, 0], dr.at[2 * yy + rr], to_row).wait_recv()
+        dkv_own[half_rows(y, r), :] += dkv_rcv[half_rows(yy, rr), :].astype(F32)
+
+    for d in range(1, ny):
+
+        @pl.when(y + d < ny)
+        def _():
+            dkv_arrival(wrap(y + d, ny), r)
+            dkv_arrival(wrap(y + d, ny), 1 - r)
+
+    dkv_arrival(y, 1 - r)
+    dp_all[0, mine, HEAD:] = dkv_own[half_rows(y, r), :].astype(BF)
+
+    peers = [to_cols[2], to_diag, to_row]
+    slots = [(2, r), (2, 1 - r), (0, 1 - r)]
+    lanes_of_part = [pl.ds(HEAD, 2 * HEAD), pl.ds(0, HEAD)]
+
+    def dp_ref(col, rr, part):
+        return dp_all.at[col, dp_rows(rr), lanes_of_part[part]]
+
+    def dp_copy(i, part):
+        return remote(
+            dp_ref(0, r, part),
+            dp_ref((2, 2, 0, 1)[i], r, part),
+            gs.at[part, i],
+            gr.at[part, i],
+            to_cols[1] if i == 3 else peers[i],
+        )
+
+    def dp_relay(i, part):
+        col, rr = slots[i]
+        return remote(
+            dp_ref(col, rr, part),
+            dp_ref(col + 1, rr, part),
+            gs.at[part, 4 + i],
+            gr.at[part, 4 + i],
+            to_cols[1],
+        )
+
+    def dp_arrival(i, part):
+        col, rr = (1, r) if i == 3 else slots[i % 4]
+        ref = dp_ref(col + 1 if i > 3 else col, rr, part)
+        remote(ref, ref, gs.at[part, i], gr.at[part, i], to_cols[1]).wait_recv()
+
+    for i in range(4):
+        go(dp_copy(i, 0))
+    dq_sum = dq_snd[z].astype(F32)
+    for d in order:
+        z_give_arrival(4, dq_rcv, d)
+        dq_sum = dq_sum + dq_rcv[wrap(z - d, nz)].astype(F32)
+    dp_all[0, mine, :HEAD] = dq_sum.T.astype(BF)
+    for i in range(4):
+        go(dp_copy(i, 1))
+
+    for t in range(2, yl + 1):
+        for round_columns in columns:
+            for column in round_columns:
+                y_round(*w_column(*column), t)
+    sib_w.wait_recv()
+
+    blk = min(512, depth)
+
+    def dx_add(i, rows, first=False, last=False):
+        def turn(j, carry):
+            start = pl.multiple_of(j * blk, blk)
+            out = pl.ds(start, blk)
+            weight = wv[pl.ds(c * depth + start, blk), :] if i == 0 else w_x[i - 1, out, :]
+            acc = dot_nt(dp_all[i, rows, :], weight)
+            if not first:
+                acc = acc + dx_acc[rows, out]
+            if last:
+                dx_ref[rows, out] = acc.astype(BF)
+            else:
+                dx_acc[rows, out] = acc
+            return carry
+
+        lax.fori_loop(0, depth // blk, turn, 0)
+
+    dx_add(0, mine, first=True)
+    dp_arrival(3, 0)
+    dp_arrival(3, 1)
+    dx_add(1, mine)
+    for part in range(2):
+        for i in range(3):
+            dp_arrival(i, part)
+            go(dp_relay(i, part))
     for i in range(1, 4):
         remote(att_all.at[i], att_all.at[i], cs.at[1, i], cr.at[1, i], to_cols[i]).wait_recv()
     for j in range(4):
@@ -659,92 +773,13 @@
                 att_all[i], wo_v[i, :, lanes], preferred_element_type=F32
             )
         out_ref[:, lanes] = total_out.astype(BF)
-
-    def dp_rows(rr):
-        return pl.ds(pl.multiple_of(rr * HEAD, HEAD), HEAD)
-
-    mine = dp_rows(r)
-    dq_sum = dq_snd[z].astype(F32)
-    for d in order:
-        z_give_arrival(4, dq_rcv, d)
-        dq_sum = dq_sum + dq_rcv[wrap(z - d, nz)].astype(F32)
-    dp_all[0, mine, :HEAD] = dq_sum.T.astype(BF)
-
-    def dkv_arrival(yy, rr):
-        ref = dkv_rcv.at[half_rows(yy, rr)]
-        remote(ref, ref, ds.at[0, 0], dr.at[2 * yy + rr], to_row).wait_recv()
-        dkv_own[half_rows(y, r), :] += dkv_rcv[half_rows(yy, rr), :].astype(F32)
-
-    dkv_arrival(y, 1 - r)
-    for d in range(1, ny):
-
-        @pl.when(y + d < ny)
-        def _():
-            dkv_arrival(wrap(y + d, ny), r)
-            dkv_arrival(wrap(y + d, ny), 1 - r)
-
-    dp_all[0, mine, HEAD:] = dkv_own[half_rows(y, r), :].astype(BF)
-
-    peers = [to_cols[2], to_row, to_diag]
-    slots = [(2, r), (0, 1 - r), (2, 1 - r)]
-
-    def dp_copy(i):
-        dst = dp_all.at[(2, 0, 2, 1)[i], mine]
-        return remote(
-            dp_all.at[0, mine], dst, gs.at[i], gr.at[i], to_cols[1] if i == 3 else peers[i]
-        )
-
-    def dp_relay(i):
-        col, rr = slots[i]
-        return remote(
-            dp_all.at[col, dp_rows(rr)],
-            dp_all.at[col + 1, dp_rows(rr)],
-            gs.at[4 + i],
-            gr.at[4 + i],
-            to_cols[1],
-        )
-
-    def dp_arrival(i):
-        col, rr = (1, r) if i == 3 else slots[i % 4]
-        col = col + 1 if i > 3 else col
-        ref = dp_all.at[col, dp_rows(rr)]
-        remote(ref, ref, gs.at[i], gr.at[i], to_cols[1]).wait_recv()
-
-    for i in (2, 1, 0, 3):
-        go(dp_copy(i))
-
-    for t in range(2, yl + 1):
-        for round_columns in columns:
-            for column in round_columns:
-                y_round(*w_column(*column), t)
-    sib_w.wait_recv()
-
-    def dx_half(rr):
-        rows = dp_rows(rr)
-        blk = min(256, depth)
-
-        def turn(j, carry):
-            start = pl.multiple_of(j * blk, blk)
-            acc = dot_nt(dp_all[0, rows, :], wv[pl.ds(c * depth + start, blk), :])
-            for i in range(1, 4):
-                acc = acc + dot_nt(dp_all[i, rows, :], w_x[i - 1, pl.ds(start, blk), :])
-            dx_ref[rows, pl.ds(start, blk)] = acc.astype(BF)
-            return carry
-
-        lax.fori_loop(0, depth // blk, turn, 0)
-
-    dp_arrival(0)
-    go(dp_relay(0))
-    dp_arrival(1)
-    go(dp_relay(1))
-    dp_arrival(2)
-    go(dp_relay(2))
-    dp_arrival(3)
-    dp_arrival(4)
-    dx_half(r)
-    dp_arrival(5)
-    dp_arrival(6)
-    dx_half(1 - r)
+    dx_add(2, mine)
+    dx_add(0, theirs, first=True)
+    dx_add(2, theirs)
+    for i, col, rows, last in ((4, 3, mine, True), (6, 1, theirs, False), (5, 3, theirs, True)):
+        dp_arrival(i, 0)
+        dp_arrival(i, 1)
+        dx_add(col, rows, last=last)
 
     for d in range(1, ny):
 
@@ -767,7 +802,7 @@
     for d in order:
         to = wrap(z + d, nz)
         z_give(1, o_snd, o_rcv, to).wait_send()
-        z_give(2, st_snd, st_rcv, to).wait_send()
+        st_copy(to).wait_send()
         z_give(4, dq_snd, dq_rcv, to).wait_send()
     for copy in seeds + [sib_w, sib_wo] + started:
         copy.wait_send()
@@ -812,10 +847,12 @@
             V((nk, nq), F32),
             V((nz, HEAD, HEAD), BF),
             V((nz, HEAD, HEAD), BF),
-            V((nz, 8, HEAD), F32),
-            V((nz, 8, HEAD), F32),
-            V((8, HEAD), F32),
-            V((nz, 8, HEAD), F32),
+            V((3, nz, HEAD), F32),
+            V((nz, 3, nz, HEAD), F32),
+            V((8, nq), F32),
+            V((HEAD, nq), F32),
+            V((nz, nz, HEAD), F32),
+            V((nz, 16, HEAD), F32),
             V((4, HEAD, HEAD), BF),
             V((nz, HEAD, HEAD), BF),
             V((nz, HEAD, HEAD), BF),
@@ -823,6 +860,7 @@
             V((nk, 2 * HEAD), BF),
             V((nk, 2 * HEAD), BF),
             V((4, 2 * HEAD, n), BF),
+            V(tokens.shape, F32),
             sem((4,)),
             sem((3, 2)),
             sem((3, 2)),
@@ -840,8 +878,6 @@
             sem((CHUNKS // 2,)),
             sem((CHUNKS // 2, nz)),
             sem((CHUNKS // 2, nz)),
-            sem((2, zl + 1)),
-            sem((2, zl + 1)),
             sem((5, nz)),
             sem((5, nz)),
             sem((CHUNKS // 2, 2 * ny + 1)),
@@ -850,8 +886,8 @@
             sem((2, 4)),
             sem((ny, 2)),
             sem((2 * ny,)),
-            sem((7,)),
-            sem((7,)),
+            sem((2, 7)),
+            sem((2, 7)),
         ],
         compiler_params=pltpu.CompilerParams(
             collective_id=0, has_side_effects=True, vmem_limit_bytes=52 * 2**20

time: 90.7 us -> 86.1 us (0.949)
  Pallas kernels: 88.2 us -> 83.6 us
    pallas_call x1, Pallas kernels: 88.2 us -> 83.6 us  [body(): pl.pallas_call(functools.partial(layer_kernel, ny, nz), out_shape=(jax.Sh...]
where the time goes in v4:
time: 86.1 us; the launch traced here: 86 us
  Pallas kernels  83.6 us (97%)
  local copies, waits for them, and re-layouts  1.76 us (2%)
    pallas_call x1, Pallas kernels, body(): pl.pallas_call(functools.partial(layer_kernel, ny, nz), out_shape=(jax.Sh...  83.6 us
    unnamed x2, local copies, waits for them, and re-layouts  1.76 us

profile of v4, /device:TPU:1, one launch (start us, length us, event | category | flops | bytes accessed | tf_op | source)
XLA Modules:
  0.0 86.0 jit_solution(3762963609635864944)
XLA Ops:
  0.6 83.6 %layer.1 = (bf16[128,3072]{1,0:T(8,128)(2,1)S(1)}, bf16[256,1536]{1,0:T(8,128)(2,1)S(1)}) custom-call(bf16[256,1536]{1,0:T(8,128)(2,1)} %t_ref.1, bf16[6144,384]{1,0:T(8,128)(2,1)} %w_ref.1, bf16[128,12288]{1,0:T(8,128)(2,1)} %wo_ref.1, bf16[128,3072]{1,0:T(8,128)(2,1)} %do_ref.1), custom_call_target="tpu_custom_call" | custom-call | flops 6000000000 | bytes 20000000 | tf_op jit(solution)/shard_map/layer/pallas_call | solution.py:826
  84.2 0.9 %copy.8 = bf16[128,3072]{1,0:T(8,128)(2,1)} copy(bf16[128,3072]{1,0:T(8,128)(2,1)S(1)} %get-tuple-element.4) | data formatting | bytes 1572864
  85.1 0.9 %copy.9 = bf16[256,1536]{1,0:T(8,128)(2,1)} copy(bf16[256,1536]{1,0:T(8,128)(2,1)S(1)} %get-tuple-element.5) | data formatting | bytes 1572864

commit v5 on v4

--- a/solution.py
+++ b/solution.py
@@ -77,6 +77,7 @@
     do_v,
     ups,
     upr,
+    up_own,
     s_all,
     o_snd,
     o_rcv,
@@ -210,7 +211,7 @@
             )
         )
     seeds = w_seeds + o_seeds + o_direct
-    for copy in w_seeds + o_seeds:
+    for copy in w_seeds + o_seeds + o_direct:
         copy.start()
 
     def rows_of(k):
@@ -235,9 +236,6 @@
         token_copy(0, k).start()
     for k in range(CHUNKS):
         token_copy(1, k).start()
-    for copy in o_direct:
-        copy.start()
-
     sib_w = remote(
         w_ref.at[pl.ds(pl.multiple_of(cols[1] * depth, 16), depth), :],
         w_x.at[0],
@@ -431,6 +429,19 @@
         kv_sends(0, k)
         for d in order:
             go(q_send(d, k))
+
+    def upstream_terms():
+        own_do.wait()
+        own_wo.wait()
+        for copy in o_direct:
+            copy.wait_recv()
+        for i in (2, 3):
+            ups[i] = dot_nt(do_v[...], wo_v[i])
+            go(remote(ups.at[i], upr.at[i], cs.at[0, i], cr.at[0, i], to_cols[i]))
+        sib_wo.wait_recv()
+        ups[1] = dot_nt(do_v[...], wo_v[1])
+        go(remote(ups.at[1], upr.at[1], cs.at[0, 1], cr.at[0, 1], to_cols[1]))
+        up_own[...] = dot_nt(do_v[...], wo_v[0])
 
     for copy in w_seeds:
         copy.wait_recv()
@@ -457,26 +468,28 @@
             project_relay(k)
             if k + AHEAD < CHUNKS:
                 token_copy(0, k + AHEAD).start()
+            if k == CHUNKS - 1:
+                upstream_terms()
             project(k)
         if hk <= k < CHUNKS:
             share(k - hk)
 
-    for column in columns[zl]:
-        y_round(*w_column(*column), 1)
-
     for k in range(hk):
         kv_row_arrival(k).wait_recv()
         kv_sends(1, k)
 
-    own_do.wait()
-    own_wo.wait()
-    sib_wo.wait_recv()
-    for copy in o_direct:
-        copy.wait_recv()
     for i in range(1, 4):
-        ups[i] = dot_nt(do_v[...], wo_v[i])
-        go(remote(ups.at[i], upr.at[i], cs.at[0, i], cr.at[0, i], to_cols[i]))
-    upr[0] = dot_nt(do_v[...], wo_v[0])
+        remote(upr.at[i], upr.at[i], cs.at[0, i], cr.at[0, i], to_cols[i]).wait_recv()
+    up = up_own[...]
+    for i in range(1, 4):
+        up = up + upr[i]
+    u_all[z_rows(z), :] = up.astype(BF)
+    for d in order:
+        to = wrap(z + d, nz)
+        rows = z_rows(z)
+        go(remote(u_all.at[rows], u_all.at[rows], zs.at[0, to], zr.at[0, z], dev_z(to)))
+    for column in columns[zl]:
+        y_round(*w_column(*column), 1)
 
     for d in order:
         for k in range(hk):
@@ -544,15 +557,8 @@
         o_all[:, lanes_of] = mixed
 
     top_far = score(far, True)
-
-    for i in range(1, 4):
-        remote(upr.at[i], upr.at[i], cs.at[0, i], cr.at[0, i], to_cols[i]).wait_recv()
-    u_all[z_rows(z), :] = (upr[0] + upr[1] + upr[2] + upr[3]).astype(BF)
-    for d in order:
-        to = wrap(z + d, nz)
-        rows = z_rows(z)
-        go(remote(u_all.at[rows], u_all.at[rows], zs.at[0, to], zr.at[0, z], dev_z(to)))
     top_near = score(near, False)
+
     weigh(far, top_far)
     weigh(near, top_near)
 
@@ -672,7 +678,7 @@
     def dp_rows(rr):
         return pl.ds(pl.multiple_of(rr * HEAD, HEAD), HEAD)
 
-    mine, theirs = dp_rows(r), dp_rows(1 - r)
+    mine, theirs, both = dp_rows(r), dp_rows(1 - r), slice(0, 2 * HEAD)
 
     def dkv_arrival(yy, rr):
         ref = dkv_rcv.at[half_rows(yy, rr)]
@@ -722,6 +728,17 @@
 
     for i in range(4):
         go(dp_copy(i, 0))
+    for i in range(1, 4):
+        remote(att_all.at[i], att_all.at[i], cs.at[1, i], cr.at[1, i], to_cols[i]).wait_recv()
+    for j in range(4):
+        part = width // 4
+        lanes = pl.ds(j * part, part)
+        total_out = jnp.dot(att_all[0], wo_v[0, :, lanes], preferred_element_type=F32)
+        for i in range(1, 4):
+            total_out = total_out + jnp.dot(
+                att_all[i], wo_v[i, :, lanes], preferred_element_type=F32
+            )
+        out_ref[:, lanes] = total_out.astype(BF)
     dq_sum = dq_snd[z].astype(F32)
     for d in order:
         z_give_arrival(4, dq_rcv, d)
@@ -762,24 +779,15 @@
         for i in range(3):
             dp_arrival(i, part)
             go(dp_relay(i, part))
-    for i in range(1, 4):
-        remote(att_all.at[i], att_all.at[i], cs.at[1, i], cr.at[1, i], to_cols[i]).wait_recv()
-    for j in range(4):
-        part = width // 4
-        lanes = pl.ds(j * part, part)
-        total_out = jnp.dot(att_all[0], wo_v[0, :, lanes], preferred_element_type=F32)
-        for i in range(1, 4):
-            total_out = total_out + jnp.dot(
-                att_all[i], wo_v[i, :, lanes], preferred_element_type=F32
-            )
-        out_ref[:, lanes] = total_out.astype(BF)
-    dx_add(2, mine)
     dx_add(0, theirs, first=True)
-    dx_add(2, theirs)
-    for i, col, rows, last in ((4, 3, mine, True), (6, 1, theirs, False), (5, 3, theirs, True)):
-        dp_arrival(i, 0)
-        dp_arrival(i, 1)
-        dx_add(col, rows, last=last)
+    dx_add(2, both)
+    for part in range(2):
+        dp_arrival(6, part)
+    dx_add(1, theirs)
+    for part in range(2):
+        dp_arrival(4, part)
+        dp_arrival(5, part)
+    dx_add(3, both, last=True)
 
     for d in range(1, ny):
 
@@ -844,6 +852,7 @@
             V((HEAD, width), BF),
             V((4, HEAD, HEAD), F32),
             V((4, HEAD, HEAD), F32),
+            V((HEAD, HEAD), F32),
             V((nk, nq), F32),
             V((nz, HEAD, HEAD), BF),
             V((nz, HEAD, HEAD), BF),

time: 86.1 us -> 80 us (0.929)
  Pallas kernels: 83.6 us -> 77.5 us
    pallas_call x1, Pallas kernels: 83.6 us -> 77.5 us  [body(): pl.pallas_call(functools.partial(layer_kernel, ny, nz), out_shape=(jax.Sh...]
where the time goes in v5:
time: 80 us; the launch traced here: 79.9 us
  Pallas kernels  77.5 us (97%)
  local copies, waits for them, and re-layouts  1.76 us (2%)
    pallas_call x1, Pallas kernels, body(): pl.pallas_call(functools.partial(layer_kernel, ny, nz), out_shape=(jax.Sh...  77.5 us
    unnamed x2, local copies, waits for them, and re-layouts  1.76 us

profile of v5, /device:TPU:1, one launch (start us, length us, event | category | flops | bytes accessed | tf_op | source)
XLA Modules:
  0.0 79.9 jit_solution(18121163534141816296)
XLA Ops:
  0.6 77.5 %layer.1 = (bf16[128,3072]{1,0:T(8,128)(2,1)S(1)}, bf16[256,1536]{1,0:T(8,128)(2,1)S(1)}) custom-call(bf16[256,1536]{1,0:T(8,128)(2,1)} %t_ref.1, bf16[6144,384]{1,0:T(8,128)(2,1)} %w_ref.1, bf16[128,12288]{1,0:T(8,128)(2,1)} %wo_ref.1, bf16[128,3072]{1,0:T(8,128)(2,1)} %do_ref.1), custom_call_target="tpu_custom_call" | custom-call | flops 6000000000 | bytes 20000000 | tf_op jit(solution)/shard_map/layer/pallas_call | solution.py:834
  78.2 0.9 %copy.8 = bf16[128,3072]{1,0:T(8,128)(2,1)} copy(bf16[128,3072]{1,0:T(8,128)(2,1)S(1)} %get-tuple-element.4) | data formatting | bytes 1572864
  79.0 0.9 %copy.9 = bf16[256,1536]{1,0:T(8,128)(2,1)} copy(bf16[256,1536]{1,0:T(8,128)(2,1)S(1)} %get-tuple-element.5) | data formatting | bytes 1572864

commit v6 on v5

--- a/solution.py
+++ b/solution.py
@@ -79,6 +79,7 @@
     upr,
     up_own,
     s_all,
+    pg_all,
     o_snd,
     o_rcv,
     st_snd,
@@ -585,6 +586,15 @@
         z_give(1, o_snd, o_rcv, wrap(z + d, nz)).start()
     o_rcv[z] = o_snd[z]
     st_rcv[z] = st_snd[...]
+
+    def ahead_turn(yy, carry):
+        for half in range(2):
+            lanes = slice(half * hq, (half + 1) * hq)
+            pg_all[y_rows(yy), lanes] = dot_nt(kv_all[y_rows(yy), HEAD:], u_all[lanes, :])
+            s_all[y_rows(yy), lanes] = jnp.exp(s_all[y_rows(yy), lanes] - st_rows[0:1, lanes])
+        return carry
+
+    lax.fori_loop(0, y + 1, ahead_turn, 0)
     for d in order:
         z_give_arrival(2, st_rcv, d)
     top = st_rcv[0, 0]
@@ -623,13 +633,13 @@
         lanes_of = q_half(half)
         queries, upstream = q_all[lanes_of, :], u_all[lanes_of, :]
         logsum = jnp.concatenate([ld[half * hz + j, 0:1, :] for j in range(hz)], axis=1)
+        scale = jnp.exp(st_rows[0:1, lanes_of] - logsum)
         delta = jnp.concatenate([ld[half * hz + j, 1:2, :] for j in range(hz)], axis=1)
 
         def grad_turn(yy, dq):
-            keys, values = kv_all[y_rows(yy), :HEAD], kv_all[y_rows(yy), HEAD:]
-            probs = jnp.exp(s_all[y_rows(yy), lanes_of] - logsum)
-            prob_grad = dot_nt(values, upstream)
-            score_grad = (probs * (prob_grad - delta)).astype(BF)
+            keys = kv_all[y_rows(yy), :HEAD]
+            probs = s_all[y_rows(yy), lanes_of] * scale
+            score_grad = (probs * (pg_all[y_rows(yy), lanes_of] - delta)).astype(BF)
             dk = jnp.dot(score_grad, queries, preferred_element_type=F32) * factor
             dv = jnp.dot(probs.astype(BF), upstream, preferred_element_type=F32)
             if first:
@@ -853,6 +863,7 @@
             V((4, HEAD, HEAD), F32),
             V((4, HEAD, HEAD), F32),
             V((HEAD, HEAD), F32),
+            V((nk, nq), F32),
             V((nk, nq), F32),
             V((nz, HEAD, HEAD), BF),
             V((nz, HEAD, HEAD), BF),

time: 80 us -> 79.2 us (0.990)
    pallas_call x1, Pallas kernels: 77.5 us -> 76.7 us  [body(): pl.pallas_call(functools.partial(layer_kernel, ny, nz), out_shape=(jax.Sh...]
where the time goes in v6:
time: 79.2 us; the launch traced here: 79.1 us
  Pallas kernels  76.7 us (97%)
  local copies, waits for them, and re-layouts  1.76 us (2%)
    pallas_call x1, Pallas kernels, body(): pl.pallas_call(functools.partial(layer_kernel, ny, nz), out_shape=(jax.Sh...  76.7 us
    unnamed x2, local copies, waits for them, and re-layouts  1.76 us

profile of v6, /device:TPU:1, one launch (start us, length us, event | category | flops | bytes accessed | tf_op | source)
XLA Modules:
  0.0 79.1 jit_solution(12112176105196105783)
XLA Ops:
  0.6 76.7 %layer.1 = (bf16[128,3072]{1,0:T(8,128)(2,1)S(1)}, bf16[256,1536]{1,0:T(8,128)(2,1)S(1)}) custom-call(bf16[256,1536]{1,0:T(8,128)(2,1)} %t_ref.1, bf16[6144,384]{1,0:T(8,128)(2,1)} %w_ref.1, bf16[128,12288]{1,0:T(8,128)(2,1)} %wo_ref.1, bf16[128,3072]{1,0:T(8,128)(2,1)} %do_ref.1), custom_call_target="tpu_custom_call" | custom-call | flops 6000000000 | bytes 20000000 | tf_op jit(solution)/shard_map/layer/pallas_call | solution.py:844
  77.3 0.9 %copy.8 = bf16[128,3072]{1,0:T(8,128)(2,1)} copy(bf16[128,3072]{1,0:T(8,128)(2,1)S(1)} %get-tuple-element.4) | data formatting | bytes 1572864
  78.2 0.9 %copy.9 = bf16[256,1536]{1,0:T(8,128)(2,1)} copy(bf16[256,1536]{1,0:T(8,128)(2,1)S(1)} %get-tuple-element.5) | data formatting | bytes 1572864
